TPU v7x, 256 devices: a whole 4x4x8 slice. The times are simulated.
256 devices in a mesh: dp: 32 (over y_lo, z, core), mp: 8 (over x, y_hi).
Axes of the slice: x: 4, y: 4 (y_hi: 2, y_lo: 2; y = y_hi * 2 + y_lo), z: 8, core: 2. Of those that a mesh axis runs over, the one named last changes fastest.
Arguments:
- img_features: bfloat16 [8192, 1152], P(('dp', 'mp')), may hold values from -8 to 8
- txt_features: bfloat16 [8192, 1152], P(('dp', 'mp')), may hold values from -8 to 8
- img_weight: bfloat16 [1152, 1152], P('mp'), may hold values from -1 to 1
- txt_weight: bfloat16 [1152, 1152], P('mp'), may hold values from -1 to 1
- img_bias: float32 [1152], replicated, may hold values from -2.5 to 2.5
- txt_bias: float32 [1152], replicated, may hold values from -2.5 to 2.5
- log_scale: float32 [1], replicated, may hold values from 1.8 to 2.3
- logit_bias: float32 [1], replicated, may hold values from -8 to -4
Outputs:
- mean_loss: float32 [1], replicated
- scale_grads: float32 [2], replicated
- img_feature_grad: bfloat16 [8192, 1152], P(('dp', 'mp'))
- txt_feature_grad: bfloat16 [8192, 1152], P(('dp', 'mp'))
- img_weight_grad: float32 [1152, 1152], P('mp', 'dp')
- txt_weight_grad: float32 [1152, 1152], P('mp', 'dp')
- bias_grads: float32 [2, 1152], replicated
All inputs are finite; a program needn't handle non-finite values.
Results may differ from a plain program's by a relative error of at most 0.0047.
Values may be sent and summed in bfloat16 or wider, within the bound.
A program may use at most 128 MiB of HBM per device.

v0:
```python
import jax
import jax.numpy as jnp
from jax import lax
from jax.sharding import PartitionSpec as P

epsilon = 1e-06
LOSS_FACTOR = 32.0


def passed_along(block, axis, distance):
    devices = range(lax.axis_size(axis))
    route = [((i - distance) % len(devices), i) for i in devices]
    return lax.ppermute(block, axis, route)


def project_rows(features, weight, bias):
    pre = jnp.dot(features, weight, preferred_element_type=jnp.float32) + bias
    inverse = lax.rsqrt(jnp.sum(pre * pre, axis=1, keepdims=True) + epsilon)
    unit = pre * inverse
    return (unit, inverse, unit.astype(jnp.bfloat16))


def norm_backward(grad, unit, inverse):
    return inverse * (grad - unit * jnp.sum(unit * grad, axis=1, keepdims=True))


def per_device(
    img_features, txt_features, img_weight, txt_weight, img_bias, txt_bias, log_scale, logit_bias
):
    w_img, w_txt = (
        lax.all_gather(img_weight, "mp", axis=0, tiled=True),
        lax.all_gather(txt_weight, "mp", axis=0, tiled=True),
    )
    unit_img, inv_img, emb_img = project_rows(img_features, w_img, img_bias)
    unit_txt, inv_txt, emb_txt = project_rows(txt_features, w_txt, txt_bias)
    images = lax.all_gather(emb_img, "mp", axis=0, tiled=True)
    logit_scale = jnp.exp(log_scale[0])
    logit_shift = logit_bias[0]
    own_rows = emb_txt.shape[0]
    group_rows = images.shape[0]
    data_size = lax.axis_size("dp")
    model_size = lax.axis_size("mp")
    model_index = lax.axis_index("mp")
    col_index = jnp.arange(group_rows, dtype=jnp.int32)[None, :]

    def pair_tile(text_block, target):
        logits = (
            logit_scale
            * jnp.einsum("te,re->tr", text_block, images, preferred_element_type=jnp.float32)
            + logit_shift
        )
        errors = jax.nn.sigmoid(logits) - target
        weights = (LOSS_FACTOR * errors).astype(jnp.bfloat16)
        text_part = logit_scale * jnp.dot(weights, images, preferred_element_type=jnp.float32)
        image_part = logit_scale * jnp.einsum(
            "tr,te->re", weights, text_block, preferred_element_type=jnp.float32
        )
        pair_loss = jax.nn.softplus(-(2.0 * target - 1.0) * logits)
        stat_part = jnp.stack(
            [
                jnp.sum(pair_loss),
                LOSS_FACTOR * jnp.sum(errors * (logits - logit_shift)),
                LOSS_FACTOR * jnp.sum(errors),
            ]
        )
        return (text_part, image_part, stat_part)

    row_index = jnp.arange(own_rows, dtype=jnp.int32)[:, None] + model_index * own_rows
    diag_mask = (col_index == row_index).astype(jnp.float32)

    def cycle_turn(turn_index, loop_state):
        text_block, carried_grad, image_grad, statistics = loop_state
        home_flag = (turn_index == 0).astype(jnp.float32)
        text_part, image_part, stat_part = pair_tile(text_block, diag_mask * home_flag)
        text_block, carried_grad = (
            passed_along(text_block.astype(jnp.float32), "dp", 1).astype(text_block.dtype),
            passed_along(carried_grad + text_part, "dp", 1),
        )
        return (text_block, carried_grad, image_grad + image_part, statistics + stat_part)

    start_state = (
        emb_txt,
        jnp.zeros(emb_txt.shape, jnp.float32),
        jnp.zeros(images.shape, jnp.float32),
        jnp.zeros((3,), jnp.float32),
    )
    text_block, carried_grad, image_grad, statistics = lax.fori_loop(
        0, data_size - 1, cycle_turn, start_state
    )
    last_flag = 0.0
    text_part, image_part, stat_part = pair_tile(text_block, diag_mask * last_flag)
    text_grad = passed_along(carried_grad + text_part, "dp", 1)
    image_grad = image_grad + image_part
    statistics = statistics + stat_part
    image_own = lax.psum_scatter(image_grad, "mp", scatter_dimension=0, tiled=True)
    delta_img = norm_backward(image_own, unit_img, inv_img)
    delta_txt = norm_backward(text_grad, unit_txt, inv_txt)
    delta_img16 = delta_img.astype(jnp.bfloat16)
    delta_txt16 = delta_txt.astype(jnp.bfloat16)
    img_feature_grad = jnp.einsum(
        "te,de->td", delta_img16, w_img, preferred_element_type=jnp.float32
    ).astype(jnp.bfloat16)
    txt_feature_grad = jnp.einsum(
        "te,de->td", delta_txt16, w_txt, preferred_element_type=jnp.float32
    ).astype(jnp.bfloat16)
    weight_term = jnp.stack(
        [
            jnp.einsum("td,te->de", img_features, delta_img16, preferred_element_type=jnp.float32),
            jnp.einsum("td,te->de", txt_features, delta_txt16, preferred_element_type=jnp.float32),
        ],
        axis=1,
    )
    reduced = lax.psum_scatter(weight_term, "dp", scatter_dimension=2, tiled=True)
    reduced = lax.psum_scatter(reduced, "mp", scatter_dimension=0, tiled=True)
    bias_local = jnp.stack([jnp.sum(delta_img, axis=0), jnp.sum(delta_txt, axis=0)])
    stat_total, bias_grads = lax.psum((statistics, bias_local), ("dp", "mp"))
    batch_rows = own_rows * data_size * model_size
    mean_loss = stat_total[0:1] / batch_rows
    scale_grads = stat_total[1:3]
    return (
        mean_loss,
        scale_grads,
        img_feature_grad,
        txt_feature_grad,
        reduced[:, 0, :],
        reduced[:, 1, :],
        bias_grads,
    )


def solution(mesh):
    in_specs = (
        P(("dp", "mp"), None),
        P(("dp", "mp"), None),
        P("mp", None),
        P("mp", None),
        P(),
        P(),
        P(),
        P(),
    )
    out_specs = (
        P(),
        P(),
        P(("dp", "mp"), None),
        P(("dp", "mp"), None),
        P("mp", "dp"),
        P("mp", "dp"),
        P(),
    )
    return jax.shard_map(
        per_device, mesh=mesh, in_specs=in_specs, out_specs=out_specs, check_vma=False
    )
```

profile of v0, /device:TPU:1, one launch (start us, length us, event | category | flops | bytes accessed | tf_op | source)
XLA Modules:
  0.0 903.2 jit_solution(14919163556594304421)
XLA Ops:
  10.1 67.9 %all-gather.3.cloned.1.call-done = bf16[1152,1152]{1,0:T(8,128)(2,1)} async-done(((bf16[144,1152]{1,0:T(8,128)(2,1)}), bf16[1152,1152]{1,0:T(8,128)(2,1)}) %all-gather.3.cloned.1.call-update) | async-done | bytes 2654224 | tf_op jit(solution)/shard_map/all_gather | solution.py:32
  78.0 2.4 multiply_reduce_fusion.4
  80.5 63.2 %all-gather.5.cloned.1.call-done = bf16[1152,1152]{1,0:T(8,128)(2,1)} async-done(((bf16[144,1152]{1,0:T(8,128)(2,1)}), bf16[1152,1152]{1,0:T(8,128)(2,1)}) %all-gather.5.cloned.1.call-update) | async-done | bytes 2654224 | tf_op jit(solution)/shard_map/all_gather | solution.py:31
  143.7 2.4 multiply_reduce_fusion.3
  146.2 29.1 %all_gather.11 = bf16[256,1152]{1,0:T(8,128)(2,1)S(1)} all-gather(bf16[32,1152]{1,0:T(8,128)(2,1)S(1)} %multiply_convert_fusion.3), channel_id=1, replica_groups=mesh['dp'=32,'mp'=8] {'mp'}, dimensions={0}, use_global_device_ids=true | all-gather | bytes 663552 | tf_op jit(solution)/shard_map/all_gather | solution.py:36
  175.4 268.9 %while.22 = (s32[]{:T(128)}, bf16[32,1152]{1,0:T(8,128)(2,1)S(1)}, f32[32,1152]{1,0:T(8,128)S(1)}, f32[256,1152]{1,0:T(8,128)S(1)}, f32[3]{0:T(128)S(1)}, /*inde...) while((s32[]{:T(128)}, bf16[32,1152]{1,0:T(8,128)(2,1)S(1)}, ...), condition=%wide.region_6.7_spmd.clone, body=%wide.region_2.6_spmd.clone.sunk | while | flops 57901072 | bytes 5112505 | solution.py:87
  175.4 8.7 collective-permute-start
  209.6 2.0 collective-permute-done.1
  218.2 2.0 collective-permute-done.1
  224.8 2.0 collective-permute-done
  226.8 2.0 collective-permute-done.1
  235.5 2.0 collective-permute-done.1
  242.0 2.0 collective-permute-done
  244.1 2.0 collective-permute-done.1
  250.7 2.0 collective-permute-done
  252.7 2.0 collective-permute-done.1
  259.3 2.0 collective-permute-done
  261.3 2.0 collective-permute-done.1
  267.9 2.0 collective-permute-done
  269.9 2.0 collective-permute-done.1
  278.6 2.0 collective-permute-done.1
  285.1 2.0 collective-permute-done
  287.2 2.0 collective-permute-done.1
  293.8 2.0 collective-permute-done
  295.8 2.0 collective-permute-done.1
  302.4 2.0 collective-permute-done
  304.4 2.0 collective-permute-done.1
  311.0 2.0 collective-permute-done
  313.0 2.0 collective-permute-done.1
  321.6 2.0 collective-permute-done.1
  328.2 2.0 collective-permute-done
  330.3 2.0 collective-permute-done.1
  336.9 2.0 collective-permute-done
  338.9 2.0 collective-permute-done.1
  345.5 2.0 collective-permute-done
  347.5 2.0 collective-permute-done.1
  354.1 2.0 collective-permute-done
  356.1 2.0 collective-permute-done.1
  364.7 2.0 collective-permute-done.1
  371.3 2.0 collective-permute-done
  373.4 2.0 collective-permute-done.1
  379.9 2.0 collective-permute-done
  382.0 2.0 collective-permute-done.1
  390.6 2.0 collective-permute-done.1
  397.2 2.0 collective-permute-done
  399.2 2.0 collective-permute-done.1
  407.8 2.0 collective-permute-done.1
  414.4 2.0 collective-permute-done
  416.4 2.0 collective-permute-done.1
  423.0 2.0 collective-permute-done
  425.1 2.0 collective-permute-done.1
  433.7 2.0 collective-permute-done.1
  440.3 2.0 collective-permute-done
  442.3 2.0 collective-permute-done.1
  447.0 6.7 collective-permute-done.2
  454.0 3.2 convolution_bitcast_fusion
  457.2 64.9 %reduce-scatter.5.cloned.1.call-done = f32[32,1152]{1,0:T(8,128)} async-done(((f32[256,1152]{1,0:T(8,128)}), f32[32,1152]{1,0:T(8,128)}) %reduce-scatter.5.cloned.1.call-update) | async-done | bytes 147472 | tf_op jit(solution)/shard_map/reduce_scatter | solution.py:95
  524.2 3.2 convolution_bitcast_fusion.1
  527.5 4.8 pad_maximum_fusion
  532.2 16.0 %copy.15 = f32[1152,2,1152]{0,1,2:T(2,128)} copy(f32[1152,2,1152]{0,2,1:T(8,128)S(1)} %pad_maximum_fusion) | data formatting | bytes 21233664 | tf_op jit(solution)/shard_map/stack | solution.py:106
  552.2 250.8 %all-reduce.4.cloned.1.call-done = f32[1152,2,1152]{0,1,2:T(2,128)} async-done(((f32[1152,2,1152]{0,1,2:T(2,128)}), f32[1152,2,1152]{0,1,2:T(2,128)}) %all-reduce.4.cloned.1.call-update) | async-done | bytes 10616848
  805.8 3.0 reshape.36
  808.8 3.3 convolution_convert_fusion
  812.1 78.6 %all-reduce.1 = (f32[3]{0:T(128)S(1)}, f32[2,1152]{1,0:T(2,128)}) all-reduce(f32[3]{0:T(128)S(1)} %maximum_add_fusion, f32[2,1152]{1,0:T(2,128)S(1)} %pad_maximum_fusion.1), channel_id=1, replica_groups=mesh['dp'=32,'mp'=8] {'dp','mp'}, use_global_device_ids=true, to_apply=%region_10.11 | all-reduce | flops 2307 | bytes 18456 | tf_op jit(solution)/shard_map/psum | solution.py:116
  (281 shorter events, 139.5 us)
Async XLA Ops:
  7.2 70.8 %all-gather.3.cloned.1.call-start = ((), (), s32[]{:S(2)}) async-start(), calls=%async_computation.2 | async-start | bytes 2985984 | tf_op jit(solution)/shard_map/all_gather | solution.py:32
  7.9 135.7 %all-gather.5.cloned.1.call-start = ((), (), s32[]{:S(2)}) async-start(), calls=%async_computation.3 | async-start | bytes 2985984 | tf_op jit(solution)/shard_map/all_gather | solution.py:31
  8.7 513.4 %reduce-scatter.5.cloned.1.call-start = ((), (), s32[]{:S(2)}) async-start(), calls=%async_computation.4 | async-start | bytes 1327104 | tf_op jit(solution)/shard_map/reduce_scatter | solution.py:95
  175.4 13.2 %collective-permute-start = (bf16[32,1152]{1,0:T(8,128)(2,1)S(1)}, bf16[32,1152]{1,0:T(8,128)(2,1)S(1)}, u32[]{:S(2)}, u32[]{:S(2)}) collective-permute-start(bf16[32,1152]{1,0:T(8,128)(2,1)S(1)} %copy.28), channel_id=1, source_target_pairs={{248,0},{0,8},{8,16},{16,24},{24,32},{32,40},{40,48},{48,56},{56,6... | collective-permute-start | bytes 221192 | tf_op jit(solution)/shard_map/while/body/eval_jaxpr/ppermute | solution.py:13
  188.7 6.5 collective-permute-start
  195.2 6.5 collective-permute-start
  203.0 6.6 collective-permute-start
  211.7 6.6 collective-permute-start
  213.8 6.5 collective-permute-start.1
  220.3 6.6 collective-permute-start
  222.1 6.8 collective-permute-start.1
  228.9 6.6 collective-permute-start
  230.7 6.8 collective-permute-start.1
  237.5 6.6 collective-permute-start
  239.4 6.8 collective-permute-start.1
  246.1 6.6 collective-permute-start
  248.0 6.8 collective-permute-start.1
  254.7 6.6 collective-permute-start
  256.6 6.8 collective-permute-start.1
  263.4 6.6 collective-permute-start
  265.2 6.8 collective-permute-start.1
  272.0 6.6 collective-permute-start
  273.8 6.8 collective-permute-start.1
  280.6 6.6 collective-permute-start
  282.5 6.8 collective-permute-start.1
  289.2 6.6 collective-permute-start
  291.1 6.8 collective-permute-start.1
  297.8 6.6 collective-permute-start
  299.7 6.8 collective-permute-start.1
  306.5 6.6 collective-permute-start
  308.3 6.8 collective-permute-start.1
  315.1 6.6 collective-permute-start
  316.9 6.8 collective-permute-start.1
  323.7 6.6 collective-permute-start
  325.5 6.8 collective-permute-start.1
  332.3 6.6 collective-permute-start
  334.2 6.8 collective-permute-start.1
  340.9 6.6 collective-permute-start
  342.8 6.8 collective-permute-start.1
  349.5 6.6 collective-permute-start
  351.4 6.8 collective-permute-start.1
  358.2 6.6 collective-permute-start
  360.0 6.8 collective-permute-start.1
  366.8 6.6 collective-permute-start
  368.6 6.8 collective-permute-start.1
  375.4 6.6 collective-permute-start
  377.3 6.8 collective-permute-start.1
  384.0 6.6 collective-permute-start
  385.9 6.8 collective-permute-start.1
  392.6 6.6 collective-permute-start
  394.5 6.8 collective-permute-start.1
  401.3 6.6 collective-permute-start
  403.1 6.8 collective-permute-start.1
  409.9 6.6 collective-permute-start
  411.7 6.8 collective-permute-start.1
  418.5 6.6 collective-permute-start
  420.3 6.8 collective-permute-start.1
  427.1 6.6 collective-permute-start
  429.0 6.8 collective-permute-start.1
  435.7 6.6 collective-permute-start
  437.6 6.8 collective-permute-start.1
  446.7 356.2 %all-reduce.4.cloned.1.call-start = ((), (), s32[]{:S(2)}) async-start(), calls=%async_computation.6 | async-start | bytes 21233664
  447.0 6.8 collective-permute-start.2
  548.3 344.7 %reduce-scatter.7.cloned.1.call-start = ((), (), s32[]{:S(2)}) async-start(), calls=%async_computation.5 | async-start | bytes 663552
  (9 other events, 445.1 us)
Sparse Core Ops, SparseCore 0:
  10.7 67.2 all-gather.2
  80.7 62.9 all-gather.4
  446.8 75.2 reduce-scatter.4
  548.4 254.5 all-reduce.3
  808.9 73.9 reduce-scatter.6
where the time goes:
time: 905 us; the launch traced here: 903 us
  waiting for transfers between devices  569 us (63%)
  blocking collectives  108 us (12%)
  matrix products  92.7 us (10%)
  loops' own time  41.4 us (5%)
  other arithmetic  30.8 us (3%)
  local copies, waits for them, and re-layouts  26.4 us (3%)
  between operations  18.4 us (2%)
  starting transfers between devices  17.1 us (2%)
    unnamed x7, waiting for transfers between devices  252 us
    ppermute x63, waiting for transfers between devices, passed_along(): return lax.ppermute(block, axis, route)  120 us
    psum x1, blocking collectives, per_device(): stat_total, bias_grads = lax.psum((statistics, bias_local), ('dp', 'mp'))  78.6 us
    all_gather x1, waiting for transfers between devices, per_device(): lax.all_gather(txt_weight, 'mp', axis=0, tiled=True)  67.9 us
    reduce_scatter x1, waiting for transfers between devices, per_device(): lax.psum_scatter(image_grad, 'mp', scatter_dimension=0, tiled=True)  64.9 us
    all_gather x1, waiting for transfers between devices, per_device(): lax.all_gather(img_weight, 'mp', axis=0, tiled=True)  63.2 us
    dot_general x32, matrix products, pair_tile(): jnp.einsum('te,re->tr', text_block, images, preferred_element_type=jnp.fl...  50.2 us
    another operation x1, loops' own time, per_device(): lax.fori_loop(0, data_size - 1, cycle_turn, start_state)  41.4 us
  transfers between devices with their start and end apart: 68, of which 62 were waited for; matrix products, arithmetic and copies ran while one was open for 12% of the time, Pallas kernels for 0%

commit v1 on v0

v1 whole, which is shorter than its diff:
```python
import functools

import jax
import jax.numpy as jnp
from jax import lax
from jax.experimental import pallas as pl
from jax.experimental.pallas import tpu as pltpu
from jax.sharding import PartitionSpec as P

EPSILON = 1e-06
LOSS_FACTOR = 32.0
NX, NY, NZ = 4, 4, 8
ROWS = 32
D = 1152
E = 1152
SHARD = 144
KX = 2 * SHARD
MESH = pl.DeviceIdType.MESH
F32 = jnp.float32
BF16 = jnp.bfloat16

N_COPIES = 128


class Links:
    def __init__(self, send_sems, recv_sems):
        dp, mp = lax.axis_index("dp"), lax.axis_index("mp")
        self.x, self.y = mp // 2, (mp % 2) * 2 + dp // 16
        self.z, self.c = (dp // 2) % NZ, dp % 2
        self.send_sems, self.recv_sems = send_sems, recv_sems
        self.started = []

    def at(self, dx=0, dy=0, dz=0, dc=0):
        x, y = (self.x + dx) % NX, (self.y + dy) % NY
        z, c = (self.z + dz) % NZ, (self.c + dc) % 2
        return ((y % 2) * 16 + z * 2 + c, x * 2 + y // 2)

    def send(self, src, dst, device):
        k = len(self.started)
        copy = pltpu.make_async_remote_copy(
            src_ref=src,
            dst_ref=dst,
            send_sem=self.send_sems.at[k],
            recv_sem=self.recv_sems.at[k],
            device_id=device,
            device_id_type=MESH,
        )
        copy.start()
        self.started.append(copy)
        return copy


def matmul(a, b):
    return lax.dot_general(a, b, (((1,), (0,)), ((), ())), preferred_element_type=F32)


def matmul_bt(a, b):
    return lax.dot_general(a, b, (((1,), (1,)), ((), ())), preferred_element_type=F32)


def matmul_at(a, b):
    return lax.dot_general(a, b, (((0,), (0,)), ((), ())), preferred_element_type=F32)


def wait_all(copies):
    for copy in copies:
        copy.wait_recv()


def kernel(
    f_img, f_txt, w_img, w_txt, b_img, b_txt, log_scale, logit_bias,
    o_loss, o_scale, o_fi, o_ft, o_wi, o_wt, o_bias,
    fs, fk, wk, po, pk, rp0, rp, unit, inv, ia, ta, wt, tg, tgx, tgs, rt, ig0, igs, ri,
    d16, dk, bp, bx, by, bz, bs, dfs, rf, g32, gy, ry, gz32, gz, rz, fin, ow,
    send_sems, recv_sems,
):
    link = Links(send_sems, recv_sems)
    x, y, z, c = link.x, link.y, link.z, link.c

    peers = [(0, 0, 0, 1)]
    peers += [(i, j, 0, 0) for i in range(NX) for j in range(NY) if (i, j) != (0, 0)]
    peers += [(i, 0, 0, 1) for i in range(1, NX)]
    peers += [(0, 0, k, 0) for k in range(1, NZ)]
    barrier = pltpu.get_barrier_semaphore()
    for p in peers:
        pl.semaphore_signal(barrier, inc=1, device_id=link.at(*p), device_id_type=MESH)

    shard = y // 2

    @pl.when(c == 0)
    def _():
        wk[shard] = w_img[...]

    @pl.when(c == 1)
    def _():
        wk[shard] = w_txt[...]

    for k in range(NX):
        fs[0, k] = f_img[:, KX * k : KX * (k + 1)]
        fs[1, k] = f_txt[:, KX * k : KX * (k + 1)]
    pl.semaphore_wait(barrier, len(peers))

    partner = jnp.where(y % 2 == 1, 1, 3)
    got_w = link.send(wk.at[shard], wk.at[shard], link.at(dy=partner))
    got_f = []
    for r in range(NX):
        for e in range(2):
            if (r, e) == (0, 0):
                fk[0] = fs[c, x]
                continue
            got_f.append(
                link.send(
                    fs.at[(c + e) % 2, (x + r) % NX],
                    fk.at[((NX - r) % NX) * 2 + e],
                    link.at(dx=r, dc=e),
                )
            )
    wait_all(got_f)
    got_w.wait_recv()

    part = matmul(fk[...].reshape(8 * ROWS, KX), wk[...].reshape(KX, E))
    rp0[0] = part[:ROWS]
    po[...] = part[ROWS : 2 * ROWS]
    pk[...] = part[2 * ROWS :].astype(BF16).reshape(6, ROWS, E)
    got_p = [link.send(po, rp0.at[1], link.at(dc=1))]
    for r in range(1, NX):
        for e in range(2):
            got_p.append(
                link.send(pk.at[(r - 1) * 2 + e], rp.at[e, NX - r - 1], link.at(dx=r, dc=e))
            )
    wait_all(got_p)
    for t, bias in enumerate((b_img, b_txt)):
        e = (c + t) % 2
        pre = rp0[e] + bias[...]
        for r in range(NX - 1):
            pre = pre + rp[e, r].astype(F32)
        inverse = lax.rsqrt(jnp.sum(pre * pre, axis=1, keepdims=True) + EPSILON)
        unit[t] = pre * inverse
        inv[t] = jnp.broadcast_to(inverse, (ROWS, 128))
    ia[0] = unit[0].astype(BF16)
    ta[0] = unit[1].astype(BF16)

    got_t = [link.send(ta.at[0], ta.at[NZ - k], link.at(dz=k)) for k in (1, 7, 2, 6, 3, 5, 4)]
    got_s = [link.send(ta.at[0], ta.at[NZ], link.at(dc=1))]
    got_i = []
    for i in range(NX):
        for j in range(NY):
            if (i, j) != (0, 0):
                slot = ((NX - i) % NX) * NY + (NY - j) % NY
                got_i.append(link.send(ia.at[0], ia.at[slot], link.at(dx=i, dy=j)))
    for copy, k in zip(got_t, (1, 7, 2, 6, 3, 5, 4)):
        copy.wait_recv()
        got_s.append(link.send(ta.at[NZ - k], ta.at[NZ + NZ - k], link.at(dc=1)))
    wait_all(got_i)

    half = NZ * ROWS
    scale = jnp.exp(jnp.full((1, 1), log_scale[0], F32))
    shift = logit_bias[0]
    images = ia[...].reshape(16 * ROWS, E)
    stats = []
    for h in range(2):
        if h == 1:
            wait_all(got_s)
        texts = ta[NZ * h : NZ * (h + 1)].reshape(half, E)
        scaled = scale * matmul_bt(texts, images)
        logits = scaled + shift
        signed = logits
        if h == 0:
            row = lax.broadcasted_iota(jnp.int32, logits.shape, 0)
            col = lax.broadcasted_iota(jnp.int32, logits.shape, 1)
            match = jnp.logical_and(row == col, col < ROWS)
            signed = jnp.where(match, -logits, logits)
        small = jnp.exp(-jnp.abs(logits))
        loss = jnp.maximum(signed, 0.0) + jnp.log1p(small)
        errors = jnp.where(logits >= 0.0, 1.0, small) / (1.0 + small)
        if h == 0:
            errors = errors - match.astype(F32)
        weights = (LOSS_FACTOR * errors).astype(BF16)
        sums = (loss, LOSS_FACTOR * errors * scaled, LOSS_FACTOR * errors)
        stats.append([jnp.sum(v, axis=0, keepdims=True) for v in sums])
        wt[:, half * h : half * (h + 1)] = weights.T
        grad = matmul(weights, images)
        if h == 0:
            tg[...] = grad.reshape(NZ, ROWS, E)
        else:
            tgx[...] = grad.reshape(NZ, ROWS, E)
    got_x = link.send(tgx, tgs, link.at(dc=1))

    texts = ta[...].reshape(16 * ROWS, E)
    got_ig = []
    for q in range(4):
        grad = matmul(wt[128 * q : 128 * (q + 1), :], texts).reshape(4, ROWS, E)
        if q == 0:
            ig0[...] = grad[0]
        igs[4 * q : 4 * (q + 1)] = grad.astype(BF16)
        for slot in range(4 * q, 4 * q + 4):
            if slot:
                got_ig.append(
                    link.send(igs.at[slot], ri.at[slot - 1], link.at(dx=slot // 4, dy=slot % 4))
                )
        if q == 0:
            got_x.wait_recv()
            tg[...] = tg[...] + tgs[...]
            tgx16 = tg[1:].astype(BF16)
            rt[1, ...] = tgx16
            got_tg = [
                link.send(rt.at[1, k - 1], rt.at[0, k - 1], link.at(dz=k))
                for k in (4, 3, 5, 2, 6, 1, 7)
            ]

    wait_all(got_tg)
    grad_txt = tg[0]
    for k in range(NZ - 1):
        grad_txt = grad_txt + rt[0, k].astype(F32)
    wait_all(got_ig)
    grad_img = ig0[...]
    for k in range(NX * NY - 1):
        grad_img = grad_img + ri[k].astype(F32)
    for t, grad in enumerate((grad_img, grad_txt)):
        grad = scale * grad
        delta = inv[t, :, 0:1] * (grad - unit[t] * jnp.sum(unit[t] * grad, axis=1, keepdims=True))
        d16[t] = delta.astype(BF16)
        total = jnp.sum(delta, axis=0, keepdims=True)
        for k in range(9):
            bp[9 * t + k : 9 * t + k + 1, :] = total[:, 128 * k : 128 * (k + 1)]
    for k in range(3):
        lanes = stats[0][k] + stats[1][k]
        bp[18 + k : 19 + k, :] = (
            lanes[:, 0:128] + lanes[:, 128:256] + lanes[:, 256:384] + lanes[:, 384:512]
        )
    bp[21:24, :] = jnp.zeros((3, 128), F32)

    got_d = []
    for r in range(NX):
        for e in range(2):
            if (r, e) == (0, 0):
                dk[0] = d16[c]
                continue
            got_d.append(
                link.send(
                    d16.at[(c + e) % 2], dk.at[((NX - r) % NX) * 2 + e], link.at(dx=r, dc=e)
                )
            )
    got_b = [link.send(bp, bx.at[r - 1], link.at(dx=r)) for r in range(1, NX)]
    wait_all(got_d)

    deltas = dk[...].reshape(8 * ROWS, E)
    grad_w = matmul_at(fk[...].reshape(8 * ROWS, KX), deltas)
    for j in range(NY):
        part = grad_w[SHARD * (j // 2) : SHARD * (j // 2 + 1), (E // 2) * (j % 2) : (E // 2) * (j % 2 + 1)]
        g32[j] = part
        gy[j] = part.astype(BF16)
    got_y = [link.send(gy.at[(y + j) % NY], ry.at[j - 1], link.at(dy=j)) for j in (2, 1, 3)]
    wait_all(got_b)
    by[0] = bp[...] + bx[0] + bx[1] + bx[2]
    got_b = [link.send(by.at[0], by.at[j], link.at(dy=j)) for j in range(1, NY)]

    grad_f = matmul_bt(deltas, wk[...].reshape(KX, E)).astype(BF16)
    dfs[...] = grad_f.reshape(8, ROWS, KX)
    got_df = []
    for r in range(NX):
        for e in range(2):
            if (r, e) == (0, 0):
                rf[0, x] = dfs[0]
                continue
            got_df.append(link.send(dfs.at[r * 2 + e], rf.at[e, x], link.at(dx=r, dc=e)))

    wait_all(got_y)
    total = g32[y]
    for j in range(NY - 1):
        total = total + ry[j].astype(F32)
    for k in range(NZ):
        part = total[:, 72 * k : 72 * (k + 1)]
        gz32[k] = part
        gz[k] = part.astype(BF16)
    got_z = [link.send(gz.at[(z + k) % NZ], rz.at[k - 1], link.at(dz=k)) for k in (4, 3, 5, 2, 6, 1, 7)]
    wait_all(got_b)
    bz[0] = by[0] + by[1] + by[2] + by[3]
    got_b = [link.send(bz.at[0], bz.at[k], link.at(dz=k)) for k in range(1, NZ)]

    wait_all(got_df)
    for t, out in enumerate((o_fi, o_ft)):
        for k in range(NX):
            out[:, KX * k : KX * (k + 1)] = rf[(c + t) % 2, k]

    wait_all(got_b)
    bias_sum = bz[0]
    for k in range(1, NZ):
        bias_sum = bias_sum + bz[k]
    bs[0] = bias_sum
    got_b = link.send(bs.at[0], bs.at[1], link.at(dc=1))

    wait_all(got_z)
    total = gz32[z]
    for k in range(NZ - 1):
        total = total + rz[k].astype(F32)
    fin[0] = total[:, :36]
    fin[1] = total[:, 36:]
    got_w = link.send(fin.at[1 - c], ow, link.at(dc=1))
    got_b.wait_recv()
    bias_sum = bs[0] + bs[1]
    for t in range(2):
        for k in range(9):
            o_bias[t : t + 1, 128 * k : 128 * (k + 1)] = bias_sum[9 * t + k : 9 * t + k + 1, :]
    o_loss[0] = jnp.sum(bias_sum[18:19, :]) * (1.0 / 8192.0)
    o_scale[0] = jnp.sum(bias_sum[19:20, :])
    o_scale[1] = jnp.sum(bias_sum[20:21, :])
    got_w.wait_recv()

    @pl.when(c == 0)
    def _():
        o_wi[...] = fin[0]
        o_wt[...] = ow[...]

    @pl.when(c == 1)
    def _():
        o_wi[...] = ow[...]
        o_wt[...] = fin[1]

    for copy in link.started:
        copy.wait_send()


def per_device(f_img, f_txt, w_img, w_txt, b_img, b_txt, log_scale, logit_bias):
    vmem = pl.BlockSpec(memory_space=pltpu.VMEM)
    smem = pl.BlockSpec(memory_space=pltpu.SMEM)
    scratch = [
        ((2, NX, ROWS, KX), BF16),
        ((8, ROWS, KX), BF16),
        ((2, SHARD, E), BF16),
        ((ROWS, E), F32),
        ((6, ROWS, E), BF16),
        ((2, ROWS, E), F32),
        ((2, NX - 1, ROWS, E), BF16),
        ((2, ROWS, E), F32),
        ((2, ROWS, 128), F32),
        ((16, ROWS, E), BF16),
        ((16, ROWS, E), BF16),
        ((512, 512), BF16),
        ((NZ, ROWS, E), F32),
        ((NZ, ROWS, E), F32),
        ((NZ, ROWS, E), F32),
        ((2, NZ - 1, ROWS, E), BF16),
        ((ROWS, E), F32),
        ((16, ROWS, E), BF16),
        ((15, ROWS, E), BF16),
        ((2, ROWS, E), BF16),
        ((8, ROWS, E), BF16),
        ((24, 128), F32),
        ((3, 24, 128), F32),
        ((4, 24, 128), F32),
        ((8, 24, 128), F32),
        ((2, 24, 128), F32),
        ((8, ROWS, KX), BF16),
        ((2, NX, ROWS, KX), BF16),
        ((NY, SHARD, E // 2), F32),
        ((NY, SHARD, E // 2), BF16),
        ((NY - 1, SHARD, E // 2), BF16),
        ((NZ, SHARD, 72), F32),
        ((NZ, SHARD, 72), BF16),
        ((NZ - 1, SHARD, 72), BF16),
        ((2, SHARD, 36), F32),
        ((SHARD, 36), F32),
    ]
    return pl.pallas_call(
        kernel,
        out_shape=(
            jax.ShapeDtypeStruct((1,), F32),
            jax.ShapeDtypeStruct((2,), F32),
            jax.ShapeDtypeStruct((ROWS, D), BF16),
            jax.ShapeDtypeStruct((ROWS, D), BF16),
            jax.ShapeDtypeStruct((SHARD, 36), F32),
            jax.ShapeDtypeStruct((SHARD, 36), F32),
            jax.ShapeDtypeStruct((2, E), F32),
        ),
        in_specs=[vmem] * 6 + [smem] * 2,
        out_specs=(smem, smem, vmem, vmem, vmem, vmem, vmem),
        scratch_shapes=[pltpu.VMEM(shape, dtype) for shape, dtype in scratch]
        + [pltpu.SemaphoreType.DMA((N_COPIES,))] * 2,
        compiler_params=pltpu.CompilerParams(
            collective_id=0, has_side_effects=True, vmem_limit_bytes=56 * 2**20
        ),
    )(f_img, f_txt, w_img, w_txt, b_img.reshape(1, E), b_txt.reshape(1, E), log_scale, logit_bias)


def solution(mesh):
    rows = P(("dp", "mp"), None)
    return jax.shard_map(
        per_device,
        mesh=mesh,
        in_specs=(rows, rows, P("mp", None), P("mp", None), P(), P(), P(), P()),
        out_specs=(P(), P(), rows, rows, P("mp", "dp"), P("mp", "dp"), P()),
        check_vma=False,
    )
```

time: 905 us -> 119 us (0.13)
  waiting for transfers between devices: 569 us -> 0 us
  Pallas kernels: 0 us -> 108 us
  blocking collectives: 108 us -> 0 us
  matrix products: 92.7 us -> 0 us
  loops' own time: 41.4 us -> 0 us
  other arithmetic: 30.8 us -> 0 us
  local copies, waits for them, and re-layouts: 26.4 us -> 6.95 us
  starting transfers between devices: 17.1 us -> 0 us
  between operations: 18.4 us -> 3.79 us
    unnamed x7 -> x0, waiting for transfers between devices: 252 us -> none
    all_gather x2 -> x0, waiting for transfers between devices: 131 us -> none  [the longest x1 67.9 us: per_device(): lax.all_gather(txt_weight, 'mp', axis=0, tiled=True)]
    ppermute x63 -> x0, waiting for transfers between devices: 120 us -> none  [passed_along(): return lax.ppermute(block, axis, route)]
    pallas_call x0 -> x1, Pallas kernels: none -> 108 us  [per_device(): pl.pallas_call(kernel, out_shape=(jax.ShapeDtypeStruct((1,), F32), jax.Sh...]
    dot_general x102 -> x0, matrix products: 92.7 us -> none  [the longest x32 50.2 us: pair_tile(): jnp.einsum('te,re->tr', text_block, images, preferred_element_type=jnp.fl...]
    psum x1 -> x0, blocking collectives: 78.6 us -> none  [per_device(): stat_total, bias_grads = lax.psum((statistics, bias_local), ('dp', 'mp'))]
    reduce_scatter x1 -> x0, waiting for transfers between devices: 64.9 us -> none  [per_device(): lax.psum_scatter(image_grad, 'mp', scatter_dimension=0, tiled=True)]
    another operation x1 -> x0, loops' own time: 41.4 us -> none  [per_device(): lax.fori_loop(0, data_size - 1, cycle_turn, start_state)]
  transfers between devices with their start and end apart: 68 -> 0, of which waited for: 62 -> 0; matrix products, arithmetic and copies ran while one was open for 12% -> 0% of each run, Pallas kernels for 0% -> 0%
where the time goes in v1:
time: 119 us; the launch traced here: 118 us
  Pallas kernels  108 us (91%)
  local copies, waits for them, and re-layouts  6.95 us (6%)
  between operations  3.79 us (3%)
    pallas_call x1, Pallas kernels, per_device(): pl.pallas_call(kernel, out_shape=(jax.ShapeDtypeStruct((1,), F32), jax.Sh...  108 us
    unnamed x16, local copies, waits for them, and re-layouts  2.74 us

profile of v1, /device:TPU:1, one launch (start us, length us, event | category | flops | bytes accessed | tf_op | source)
XLA Modules:
  0.0 118.3 jit_solution(10228718423723390599)
XLA Ops:
  0.6 0.0 copy-start.4
  1.9 1.3 %reshape.20.b_img = f32[1,1152]{1,0:T(1,128)} reshape(f32[1152]{0:T(1024)} %param.12) | data formatting | bytes 9216 | tf_op jit(solution)/shard_map/reshape | solution.py:383
  3.2 0.0 copy-done.4
  3.2 0.6 reshape.21.b_txt
  3.8 107.6 %shard_map.135 = (f32[1]{0:T(128)}, f32[2]{0:T(128)}, bf16[32,1152]{1,0:T(8,128)(2,1)}, bf16[32,1152]{1,0:T(8,128)(2,1)}, f32[144,36]{1,0:T(8,128)}, /*index=5*/f32[144,36]{1,0:T(8,128)}, f32[2,1152]{1,0:T(2,128)}) custom-call(bf16[32,1152]{1,0:T(8,128)(2,1)} %f_img.1, bf16[32,1152]{1,0:T(8,128)(2,1)} %f_txt.1, bf16[144,1152]{1,0:T(8,128)(2,1)} %w_img.1, ...), custom_call_target="tpu_custom_call" | custom-call | tf_op jit(solution)/shard_map/pallas_call | solution.py:365
  111.4 0.0 copy-start.2
  111.5 1.6 %copy.15 = f32[144,36]{0,1:T(8,128)} copy(f32[144,36]{1,0:T(8,128)} %get-tuple-element.11) | data formatting | bytes 41472 | tf_op jit(solution)/shard_map/pallas_call | solution.py:365
  113.1 0.0 copy-done.2
  113.1 0.0 copy-start.1
  113.1 0.7 copy.16
  113.8 0.0 copy-start.5
  114.5 0.0 copy-done.5
  114.5 0.5 copy.25
  115.0 0.0 copy-done.1
  115.0 0.0 copy-start
  115.0 0.6 copy.26
  115.6 0.3 copy-done
  115.9 0.0 copy-start.3
  115.9 0.6 copy.27
  116.5 0.1 copy-done.3
  116.6 0.6 copy.28
Async XLA Ops:
  0.6 2.6 %copy-start.4 = (f32[1152]{0:T(1024)S(1)}, f32[1152]{0:T(1024)}, u32[]{:S(2)}) copy-start(f32[1152]{0:T(1024)} %param.13) | copy-start | bytes 13828
  111.4 1.6 %copy-start.2 = (f32[144,36]{1,0:T(8,128)S(1)}, f32[144,36]{1,0:T(8,128)}, u32[]{:S(2)}) copy-start(f32[144,36]{1,0:T(8,128)} %get-tuple-element.12) | copy-start | bytes 62212
  113.1 1.9 %copy-start.1 = (bf16[32,1152]{1,0:T(8,128)(2,1)S(1)}, bf16[32,1152]{1,0:T(8,128)(2,1)}, u32[]{:S(2)}) copy-start(bf16[32,1152]{1,0:T(8,128)(2,1)} %get-tuple-element.23) | copy-start | bytes 221188
  113.8 0.7 copy-start.5
  115.0 0.9 copy-start
  115.9 0.7 copy-start.3

commit v2 on v1

--- a/solution.py
+++ b/solution.py
@@ -22,6 +22,11 @@
 N_COPIES = 128
 
 
+def ring(place, size):
+    steps = [place + k for k in range(size)]
+    return [place] + [jnp.where(v >= size, v - size, v) for v in steps[1:]]
+
+
 class Links:
     def __init__(self, send_sems, recv_sems):
         dp, mp = lax.axis_index("dp"), lax.axis_index("mp")
@@ -29,11 +34,17 @@
         self.z, self.c = (dp // 2) % NZ, dp % 2
         self.send_sems, self.recv_sems = send_sems, recv_sems
         self.started = []
+        self.xs = ring(self.x, NX)
+        self.ys = ring(self.y, NY)
+        self.zs = ring(self.z, NZ)
+        self.cs = ring(self.c, 2)
+        self.x_mp = [2 * v for v in self.xs]
+        self.y_mp = [v // 2 for v in self.ys]
+        self.y_dp = [(v - 2 * h) * 16 for v, h in zip(self.ys, self.y_mp)]
+        self.z_dp = [2 * v for v in self.zs]
 
     def at(self, dx=0, dy=0, dz=0, dc=0):
-        x, y = (self.x + dx) % NX, (self.y + dy) % NY
-        z, c = (self.z + dz) % NZ, (self.c + dc) % 2
-        return ((y % 2) * 16 + z * 2 + c, x * 2 + y // 2)
+        return (self.y_dp[dy] + self.z_dp[dz] + self.cs[dc], self.x_mp[dx] + self.y_mp[dy])
 
     def send(self, src, dst, device):
         k = len(self.started)
@@ -69,9 +80,9 @@
 
 def kernel(
     f_img, f_txt, w_img, w_txt, b_img, b_txt, log_scale, logit_bias,
-    o_loss, o_scale, o_fi, o_ft, o_wi, o_wt, o_bias,
+    rf, ow, o_sums,
     fs, fk, wk, po, pk, rp0, rp, unit, inv, ia, ta, wt, tg, tgx, tgs, rt, ig0, igs, ri,
-    d16, dk, bp, bx, by, bz, bs, dfs, rf, g32, gy, ry, gz32, gz, rz, fin, ow,
+    d16, dk, bp, bx, by, bz, bs, dfs, g32, gy, ry, gz32, gz, rz, fin,
     send_sems, recv_sems,
 ):
     link = Links(send_sems, recv_sems)
@@ -85,7 +96,7 @@
     for p in peers:
         pl.semaphore_signal(barrier, inc=1, device_id=link.at(*p), device_id_type=MESH)
 
-    shard = y // 2
+    shard = link.y_mp[0]
 
     @pl.when(c == 0)
     def _():
@@ -100,8 +111,10 @@
         fs[1, k] = f_txt[:, KX * k : KX * (k + 1)]
     pl.semaphore_wait(barrier, len(peers))
 
-    partner = jnp.where(y % 2 == 1, 1, 3)
-    got_w = link.send(wk.at[shard], wk.at[shard], link.at(dy=partner))
+    odd = y - 2 * shard
+    ahead, behind = link.at(dy=1), link.at(dy=3)
+    partner = tuple(jnp.where(odd == 1, u, v) for u, v in zip(ahead, behind))
+    got_w = link.send(wk.at[shard], wk.at[shard], partner)
     got_f = []
     for r in range(NX):
         for e in range(2):
@@ -110,7 +123,7 @@
                 continue
             got_f.append(
                 link.send(
-                    fs.at[(c + e) % 2, (x + r) % NX],
+                    fs.at[link.cs[e], link.xs[r]],
                     fk.at[((NX - r) % NX) * 2 + e],
                     link.at(dx=r, dc=e),
                 )
@@ -130,8 +143,8 @@
             )
     wait_all(got_p)
     for t, bias in enumerate((b_img, b_txt)):
-        e = (c + t) % 2
-        pre = rp0[e] + bias[...]
+        e = link.cs[t]
+        pre = rp0[e] + bias[...].reshape(1, E)
         for r in range(NX - 1):
             pre = pre + rp[e, r].astype(F32)
         inverse = lax.rsqrt(jnp.sum(pre * pre, axis=1, keepdims=True) + EPSILON)
@@ -154,8 +167,8 @@
     wait_all(got_i)
 
     half = NZ * ROWS
-    scale = jnp.exp(jnp.full((1, 1), log_scale[0], F32))
-    shift = logit_bias[0]
+    scale = jnp.exp(log_scale[...].reshape(1, 1))
+    shift = logit_bias[...].reshape(1, 1)
     images = ia[...].reshape(16 * ROWS, E)
     stats = []
     for h in range(2):
@@ -238,7 +251,7 @@
                 continue
             got_d.append(
                 link.send(
-                    d16.at[(c + e) % 2], dk.at[((NX - r) % NX) * 2 + e], link.at(dx=r, dc=e)
+                    d16.at[link.cs[e]], dk.at[((NX - r) % NX) * 2 + e], link.at(dx=r, dc=e)
                 )
             )
     got_b = [link.send(bp, bx.at[r - 1], link.at(dx=r)) for r in range(1, NX)]
@@ -250,7 +263,7 @@
         part = grad_w[SHARD * (j // 2) : SHARD * (j // 2 + 1), (E // 2) * (j % 2) : (E // 2) * (j % 2 + 1)]
         g32[j] = part
         gy[j] = part.astype(BF16)
-    got_y = [link.send(gy.at[(y + j) % NY], ry.at[j - 1], link.at(dy=j)) for j in (2, 1, 3)]
+    got_y = [link.send(gy.at[link.ys[j]], ry.at[j - 1], link.at(dy=j)) for j in (2, 1, 3)]
     wait_all(got_b)
     by[0] = bp[...] + bx[0] + bx[1] + bx[2]
     got_b = [link.send(by.at[0], by.at[j], link.at(dy=j)) for j in range(1, NY)]
@@ -273,15 +286,10 @@
         part = total[:, 72 * k : 72 * (k + 1)]
         gz32[k] = part
         gz[k] = part.astype(BF16)
-    got_z = [link.send(gz.at[(z + k) % NZ], rz.at[k - 1], link.at(dz=k)) for k in (4, 3, 5, 2, 6, 1, 7)]
+    got_z = [link.send(gz.at[link.zs[k]], rz.at[k - 1], link.at(dz=k)) for k in (4, 3, 5, 2, 6, 1, 7)]
     wait_all(got_b)
     bz[0] = by[0] + by[1] + by[2] + by[3]
     got_b = [link.send(bz.at[0], bz.at[k], link.at(dz=k)) for k in range(1, NZ)]
-
-    wait_all(got_df)
-    for t, out in enumerate((o_fi, o_ft)):
-        for k in range(NX):
-            out[:, KX * k : KX * (k + 1)] = rf[(c + t) % 2, k]
 
     wait_all(got_b)
     bias_sum = bz[0]
@@ -296,29 +304,29 @@
         total = total + rz[k].astype(F32)
     fin[0] = total[:, :36]
     fin[1] = total[:, 36:]
-    got_w = link.send(fin.at[1 - c], ow, link.at(dc=1))
+    got_w = link.send(fin.at[1 - c], ow.at[1], link.at(dc=1))
     got_b.wait_recv()
-    bias_sum = bs[0] + bs[1]
-    for t in range(2):
-        for k in range(9):
-            o_bias[t : t + 1, 128 * k : 128 * (k + 1)] = bias_sum[9 * t + k : 9 * t + k + 1, :]
-    o_loss[0] = jnp.sum(bias_sum[18:19, :]) * (1.0 / 8192.0)
-    o_scale[0] = jnp.sum(bias_sum[19:20, :])
-    o_scale[1] = jnp.sum(bias_sum[20:21, :])
+    o_sums[...] = bs[0] + bs[1]
     got_w.wait_recv()
-
-    @pl.when(c == 0)
-    def _():
-        o_wi[...] = fin[0]
-        o_wt[...] = ow[...]
-
-    @pl.when(c == 1)
-    def _():
-        o_wi[...] = ow[...]
-        o_wt[...] = fin[1]
+    ow[0] = fin[c]
+    wait_all(got_df)
 
     for copy in link.started:
         copy.wait_send()
+
+
+def finish(rf, ow, sums, o_loss, o_scale, o_fi, o_ft, o_wi, o_wt, o_bias):
+    c = lax.axis_index("dp") % 2
+    for t, (out_f, out_w) in enumerate(((o_fi, o_wi), (o_ft, o_wt))):
+        e = jnp.where(c == t, 0, 1)
+        for k in range(NX):
+            out_f[:, KX * k : KX * (k + 1)] = rf[e, k]
+        out_w[...] = ow[e].T
+        for k in range(9):
+            o_bias[t : t + 1, 128 * k : 128 * (k + 1)] = sums[9 * t + k : 9 * t + k + 1, :]
+    o_loss[0] = jnp.sum(sums[18:19, :]) * (1.0 / 8192.0)
+    o_scale[0] = jnp.sum(sums[19:20, :])
+    o_scale[1] = jnp.sum(sums[20:21, :])
 
 
 def per_device(f_img, f_txt, w_img, w_txt, b_img, b_txt, log_scale, logit_bias):
@@ -352,7 +360,6 @@
         ((8, 24, 128), F32),
         ((2, 24, 128), F32),
         ((8, ROWS, KX), BF16),
-        ((2, NX, ROWS, KX), BF16),
         ((NY, SHARD, E // 2), F32),
         ((NY, SHARD, E // 2), BF16),
         ((NY - 1, SHARD, E // 2), BF16),
@@ -360,27 +367,37 @@
         ((NZ, SHARD, 72), BF16),
         ((NZ - 1, SHARD, 72), BF16),
         ((2, SHARD, 36), F32),
-        ((SHARD, 36), F32),
     ]
-    return pl.pallas_call(
+    parts = pl.pallas_call(
         kernel,
+        out_shape=(
+            jax.ShapeDtypeStruct((2, NX, ROWS, KX), BF16),
+            jax.ShapeDtypeStruct((2, SHARD, 36), F32),
+            jax.ShapeDtypeStruct((24, 128), F32),
+        ),
+        in_specs=[vmem] * 8,
+        out_specs=(vmem, vmem, vmem),
+        scratch_shapes=[pltpu.VMEM(shape, dtype) for shape, dtype in scratch]
+        + [pltpu.SemaphoreType.DMA((N_COPIES,))] * 2,
+        compiler_params=pltpu.CompilerParams(
+            collective_id=0, has_side_effects=True, vmem_limit_bytes=56 * 2**20
+        ),
+    )(f_img, f_txt, w_img, w_txt, b_img, b_txt, log_scale, logit_bias)
+    loss, scale, fi, ft, wi, wt, bias = pl.pallas_call(
+        finish,
         out_shape=(
             jax.ShapeDtypeStruct((1,), F32),
             jax.ShapeDtypeStruct((2,), F32),
             jax.ShapeDtypeStruct((ROWS, D), BF16),
             jax.ShapeDtypeStruct((ROWS, D), BF16),
-            jax.ShapeDtypeStruct((SHARD, 36), F32),
-            jax.ShapeDtypeStruct((SHARD, 36), F32),
+            jax.ShapeDtypeStruct((36, SHARD), F32),
+            jax.ShapeDtypeStruct((36, SHARD), F32),
             jax.ShapeDtypeStruct((2, E), F32),
         ),
-        in_specs=[vmem] * 6 + [smem] * 2,
+        in_specs=[vmem] * 3,
         out_specs=(smem, smem, vmem, vmem, vmem, vmem, vmem),
-        scratch_shapes=[pltpu.VMEM(shape, dtype) for shape, dtype in scratch]
-        + [pltpu.SemaphoreType.DMA((N_COPIES,))] * 2,
-        compiler_params=pltpu.CompilerParams(
-            collective_id=0, has_side_effects=True, vmem_limit_bytes=56 * 2**20
-        ),
-    )(f_img, f_txt, w_img, w_txt, b_img.reshape(1, E), b_txt.reshape(1, E), log_scale, logit_bias)
+    )(*parts)
+    return loss, scale, fi, ft, wi.T, wt.T, bias
 
 
 def solution(mesh):

time: 119 us -> 112 us (0.941)
  local copies, waits for them, and re-layouts: 6.95 us -> 0 us
  Pallas kernels: 108 us -> 110 us
  between operations: 3.79 us -> 1.93 us
    unnamed x16 -> x0, local copies, waits for them, and re-layouts: 2.74 us -> none
    pallas_call x2 -> x0, local copies, waits for them, and re-layouts: 2.33 us -> none  [per_device(): pl.pallas_call(kernel, out_shape=(jax.ShapeDtypeStruct((1,), F32), jax.Sh...]
    pallas_call x1 -> x2, Pallas kernels: 108 us -> 110 us  [the longest x1 108 us: per_device(): pl.pallas_call(kernel, out_shape=(jax.ShapeDtypeStruct((2, NX, ROWS, KX),...]
    reshape x2 -> x0, local copies, waits for them, and re-layouts: 1.89 us -> none  [the longest x1 1.29 us: per_device(): b_img.reshape(1, E)]
where the time goes in v2:
time: 112 us; the launch traced here: 111 us
  Pallas kernels  110 us (98%)
  between operations  1.93 us (2%)
    pallas_call x1, Pallas kernels, per_device(): pl.pallas_call(kernel, out_shape=(jax.ShapeDtypeStruct((2, NX, ROWS, KX),...  108 us

profile of v2, /device:TPU:1, one launch (start us, length us, event | category | flops | bytes accessed | tf_op | source)
XLA Modules:
  0.0 111.5 jit_solution(14958828582033880116)
XLA Ops:
  1.9 107.7 %shard_map.135 = (bf16[2,4,32,288]{3,2,1,0:T(8,128)(2,1)}, f32[2,144,36]{2,1,0:T(8,128)}, f32[24,128]{1,0:T(8,128)}) custom-call(bf16[32,1152]{1,0:T(8,128)(2,1)} %f_img.1, bf16[32,1152]{1,0:T(8,128)(2,1)} %f_txt.1, bf16[144,1152]{1,0:T(8,128)(2,1)} %w_img.1, bf16[144,1152]{1,0:T(8,128)(2,1)} %w_txt.1, f32[1152]{0:T(1024)} %b_img.1, f32[1152]{0:T(1024)} %b_txt.1, ...), custom_call_target="tpu_custom_call" | custom-call | tf_op jit(solution)/shard_map/pallas_call | solution.py:371
  109.6 1.8 %shard_map.136 = (f32[1]{0:T(128)}, f32[2]{0:T(128)}, bf16[32,1152]{1,0:T(8,128)(2,1)}, bf16[32,1152]{1,0:T(8,128)(2,1)}, f32[36,144]{1,0:T(8,128)}, /*index=5*/f32[36,144]{1,0:T(8,128)}, f32[2,1152]{1,0:T(2,128)}) custom-call(bf16[2,4,32,288]{3,2,1,0:T(8,128)(2,1)} %get-tuple-element.17.rf, f32[2,144,36]{2,1,0:T(8,128)} %get-tuple-element.18.ow, ...), custom_call_target="tpu_custom_call" | custom-call | tf_op jit(solution)/shard_map/pallas_call | solution.py:386

commit v3 on v2

--- a/solution.py
+++ b/solution.py
@@ -11,6 +11,7 @@
 LOSS_FACTOR = 32.0
 NX, NY, NZ = 4, 4, 8
 ROWS = 32
+HALF = ROWS // 2
 D = 1152
 E = 1152
 SHARD = 144
@@ -78,20 +79,123 @@
         copy.wait_recv()
 
 
+def gather_z(link, buf, split, on_arrival):
+    to_7 = link.send(buf.at[0], buf.at[7], link.at(dz=1))
+    to_1 = link.send(buf.at[0], buf.at[1], link.at(dz=7))
+    to_6 = link.send(buf.at[0], buf.at[6], link.at(dz=2))
+    to_2 = link.send(buf.at[0], buf.at[2], link.at(dz=6))
+    yield
+    to_7.wait_recv()
+    to_5 = link.send(buf.at[7], buf.at[5], link.at(dz=2))
+    on_arrival(7)
+    yield
+    to_1.wait_recv()
+    to_3 = link.send(buf.at[1], buf.at[3], link.at(dz=6))
+    on_arrival(1)
+    yield
+    to_6.wait_recv()
+    if split is None:
+        to_4 = [link.send(buf.at[6], buf.at[4], link.at(dz=2))]
+    else:
+        to_4 = [link.send(buf.at[6, :split], buf.at[4, :split], link.at(dz=2))]
+    on_arrival(6)
+    yield
+    to_2.wait_recv()
+    if split is not None:
+        to_4.append(link.send(buf.at[2, split:], buf.at[4, split:], link.at(dz=6)))
+    on_arrival(2)
+    yield
+    to_5.wait_recv()
+    on_arrival(5)
+    to_3.wait_recv()
+    on_arrival(3)
+    wait_all(to_4)
+    on_arrival(4)
+
+
+def gather_plane(link, buf):
+    steps = (1, 3, 2)
+    top, low = pl.ds(0, HALF), pl.ds(HALF, HALF)
+    got = []
+    got_x = [link.send(buf.at[0, 0], buf.at[NX - i, 0], link.at(dx=i)) for i in steps]
+    got_y = [link.send(buf.at[0, 0], buf.at[0, NY - j], link.at(dy=j)) for j in steps]
+    yield
+    for copy_x, copy_y, k in zip(got_x, got_y, steps):
+        a = NX - k
+        copy_x.wait_recv()
+        for j in steps:
+            got.append(link.send(buf.at[a, 0, top], buf.at[a, NY - j, top], link.at(dy=j)))
+        copy_y.wait_recv()
+        for i in steps:
+            got.append(link.send(buf.at[0, a, low], buf.at[NX - i, a, low], link.at(dx=i)))
+        yield
+    wait_all(got)
+
+
+def interleave(*parts):
+    parts = list(parts)
+    while parts:
+        for part in list(parts):
+            try:
+                next(part)
+            except StopIteration:
+                parts.remove(part)
+
+
+def reduce_z_start(link, part, sent, got, split):
+    for i, k in enumerate((3, 5, 4)):
+        sent[i] = part(k).astype(BF16)
+    return [
+        link.send(sent.at[0], got.at[0], link.at(dz=2)),
+        link.send(sent.at[1], got.at[1], link.at(dz=6)),
+        link.send(sent.at[2, :split], got.at[2, :split], link.at(dz=2)),
+        link.send(sent.at[2, split:], got.at[2, split:], link.at(dz=6)),
+    ]
+
+
+def reduce_z_finish(link, part, sent, got, split, first):
+    first[0].wait_recv()
+    sent[3] = (part(1) + got[0].astype(F32)).astype(BF16)
+    last = [link.send(sent.at[3], got.at[3], link.at(dz=1))]
+    first[1].wait_recv()
+    sent[4] = (part(7) + got[1].astype(F32)).astype(BF16)
+    last.append(link.send(sent.at[4], got.at[4], link.at(dz=7)))
+    first[2].wait_recv()
+    term = part(2)
+    sent[5, :split] = (term[:split] + got[2, :split].astype(F32)).astype(BF16)
+    sent[5, split:] = term[split:].astype(BF16)
+    last.append(link.send(sent.at[5], got.at[5], link.at(dz=2)))
+    first[3].wait_recv()
+    term = part(6)
+    sent[6, :split] = term[:split].astype(BF16)
+    sent[6, split:] = (term[split:] + got[2, split:].astype(F32)).astype(BF16)
+    last.append(link.send(sent.at[6], got.at[6], link.at(dz=6)))
+    return last
+
+
+def reduce_z_sum(part, got, last):
+    total = part(0)
+    for k, copy in enumerate(last):
+        copy.wait_recv()
+        total = total + got[3 + k].astype(F32)
+    return total
+
+
 def kernel(
     f_img, f_txt, w_img, w_txt, b_img, b_txt, log_scale, logit_bias,
     rf, ow, o_sums,
-    fs, fk, wk, po, pk, rp0, rp, unit, inv, ia, ta, wt, tg, tgx, tgs, rt, ig0, igs, ri,
-    d16, dk, bp, bx, by, bz, bs, dfs, g32, gy, ry, gz32, gz, rz, fin,
+    fs, fk, wk, po, pk, rp0, rp, unit, inv, ia, ta, wt, tg, tgx, tgs, tz_sent, tz_got,
+    ig0, ig_x32, ig_y32, ig_top, ig_low, r_top, r_low, ig2_top, ig2_low, r2_top, r2_low,
+    d16, dk, bp, bx, by, bz, bs, dfs, g32, gy, ry, gz32, gz_sent, gz_got, fin,
     send_sems, recv_sems,
 ):
     link = Links(send_sems, recv_sems)
     x, y, z, c = link.x, link.y, link.z, link.c
 
     peers = [(0, 0, 0, 1)]
-    peers += [(i, j, 0, 0) for i in range(NX) for j in range(NY) if (i, j) != (0, 0)]
-    peers += [(i, 0, 0, 1) for i in range(1, NX)]
-    peers += [(0, 0, k, 0) for k in range(1, NZ)]
+    peers += [(i, 0, 0, e) for i in range(1, NX) for e in range(2)]
+    peers += [(0, j, 0, 0) for j in range(1, NY)]
+    peers += [(0, 0, k, 0) for k in (1, 2, 6, 7)]
     barrier = pltpu.get_barrier_semaphore()
     for p in peers:
         pl.semaphore_signal(barrier, inc=1, device_id=link.at(*p), device_id_type=MESH)
@@ -150,21 +254,15 @@
         inverse = lax.rsqrt(jnp.sum(pre * pre, axis=1, keepdims=True) + EPSILON)
         unit[t] = pre * inverse
         inv[t] = jnp.broadcast_to(inverse, (ROWS, 128))
-    ia[0] = unit[0].astype(BF16)
-    ta[0] = unit[1].astype(BF16)
-
-    got_t = [link.send(ta.at[0], ta.at[NZ - k], link.at(dz=k)) for k in (1, 7, 2, 6, 3, 5, 4)]
-    got_s = [link.send(ta.at[0], ta.at[NZ], link.at(dc=1))]
-    got_i = []
-    for i in range(NX):
-        for j in range(NY):
-            if (i, j) != (0, 0):
-                slot = ((NX - i) % NX) * NY + (NY - j) % NY
-                got_i.append(link.send(ia.at[0], ia.at[slot], link.at(dx=i, dy=j)))
-    for copy, k in zip(got_t, (1, 7, 2, 6, 3, 5, 4)):
-        copy.wait_recv()
-        got_s.append(link.send(ta.at[NZ - k], ta.at[NZ + NZ - k], link.at(dc=1)))
-    wait_all(got_i)
+    ia[0, 0] = unit[0].astype(BF16)
+    ta[0, 0] = unit[1].astype(BF16)
+
+    got_s = [link.send(ta.at[0, 0], ta.at[1, 0], link.at(dc=1))]
+
+    def forward(k):
+        got_s.append(link.send(ta.at[0, k], ta.at[1, k], link.at(dc=1)))
+
+    interleave(gather_z(link, ta.at[0], HALF, forward), gather_plane(link, ia))
 
     half = NZ * ROWS
     scale = jnp.exp(log_scale[...].reshape(1, 1))
@@ -174,7 +272,7 @@
     for h in range(2):
         if h == 1:
             wait_all(got_s)
-        texts = ta[NZ * h : NZ * (h + 1)].reshape(half, E)
+        texts = ta[h].reshape(half, E)
         scaled = scale * matmul_bt(texts, images)
         logits = scaled + shift
         signed = logits
@@ -197,38 +295,61 @@
             tg[...] = grad.reshape(NZ, ROWS, E)
         else:
             tgx[...] = grad.reshape(NZ, ROWS, E)
-    got_x = link.send(tgx, tgs, link.at(dc=1))
-
+    got_x = [
+        link.send(tgx.at[k], tgs.at[k], link.at(dc=1))
+        for k in (pl.ds(3, 3), pl.ds(0, 3), pl.ds(6, 2))
+    ]
+
+    def txt_part(k):
+        return tg[k] + tgs[k]
+
+    top, low = pl.ds(0, HALF), pl.ds(HALF, HALF)
     texts = ta[...].reshape(16 * ROWS, E)
-    got_ig = []
-    for q in range(4):
-        grad = matmul(wt[128 * q : 128 * (q + 1), :], texts).reshape(4, ROWS, E)
-        if q == 0:
+    got_low, got_top = [], []
+    for i, a in enumerate((2, 1, 3, 0)):
+        grad = matmul(wt[128 * a : 128 * (a + 1), :], texts).reshape(NY, ROWS, E)
+        ig_top[:, a] = grad[:, :HALF].astype(BF16)
+        ig_low[a] = grad[:, HALF:].astype(BF16)
+        if a:
+            ig_x32[a - 1] = grad[0, :HALF]
+            got_low.append(link.send(ig_low.at[a], r_low.at[a - 1], link.at(dx=a)))
+        else:
             ig0[...] = grad[0]
-        igs[4 * q : 4 * (q + 1)] = grad.astype(BF16)
-        for slot in range(4 * q, 4 * q + 4):
-            if slot:
-                got_ig.append(
-                    link.send(igs.at[slot], ri.at[slot - 1], link.at(dx=slot // 4, dy=slot % 4))
-                )
-        if q == 0:
-            got_x.wait_recv()
-            tg[...] = tg[...] + tgs[...]
-            tgx16 = tg[1:].astype(BF16)
-            rt[1, ...] = tgx16
-            got_tg = [
-                link.send(rt.at[1, k - 1], rt.at[0, k - 1], link.at(dz=k))
-                for k in (4, 3, 5, 2, 6, 1, 7)
-            ]
-
-    wait_all(got_tg)
-    grad_txt = tg[0]
-    for k in range(NZ - 1):
-        grad_txt = grad_txt + rt[0, k].astype(F32)
-    wait_all(got_ig)
-    grad_img = ig0[...]
-    for k in range(NX * NY - 1):
-        grad_img = grad_img + ri[k].astype(F32)
+            ig_y32[...] = grad[1:, HALF:]
+        if i == 0:
+            got_x[0].wait_recv()
+            first = reduce_z_start(link, txt_part, tz_sent, tz_got, HALF)
+    for j in (2, 1, 3):
+        got_top.append(link.send(ig_top.at[j], r_top.at[j - 1], link.at(dy=j)))
+    wait_all(got_x[1:])
+    got_tg = reduce_z_finish(link, txt_part, tz_sent, tz_got, HALF, first)
+
+    wait_all(got_low)
+    got_low2 = []
+    for j in (2, 1, 3):
+        total = ig_y32[j - 1]
+        for i in range(NX - 1):
+            total = total + r_low[i, j].astype(F32)
+        ig2_low[j - 1] = total.astype(BF16)
+        got_low2.append(link.send(ig2_low.at[j - 1], r2_low.at[j - 1], link.at(dy=j)))
+    wait_all(got_top)
+    got_top2 = []
+    for i in (2, 1, 3):
+        total = ig_x32[i - 1]
+        for j in range(NY - 1):
+            total = total + r_top[j, i].astype(F32)
+        ig2_top[i - 1] = total.astype(BF16)
+        got_top2.append(link.send(ig2_top.at[i - 1], r2_top.at[i - 1], link.at(dx=i)))
+
+    grad_txt = reduce_z_sum(txt_part, tz_got, got_tg)
+    wait_all(got_low2 + got_top2)
+    halves = []
+    for rows, first_got, second_got in ((top, r_top, r2_top), (low, r_low, r2_low)):
+        total = ig0[rows, :]
+        for k in range(3):
+            total = total + first_got[k, 0].astype(F32) + second_got[k].astype(F32)
+        halves.append(total)
+    grad_img = jnp.concatenate(halves, axis=0)
     for t, grad in enumerate((grad_img, grad_txt)):
         grad = scale * grad
         delta = inv[t, :, 0:1] * (grad - unit[t] * jnp.sum(unit[t] * grad, axis=1, keepdims=True))
@@ -283,25 +404,23 @@
     for j in range(NY - 1):
         total = total + ry[j].astype(F32)
     for k in range(NZ):
-        part = total[:, 72 * k : 72 * (k + 1)]
-        gz32[k] = part
-        gz[k] = part.astype(BF16)
-    got_z = [link.send(gz.at[link.zs[k]], rz.at[k - 1], link.at(dz=k)) for k in (4, 3, 5, 2, 6, 1, 7)]
+        gz32[k] = total[:, 72 * k : 72 * (k + 1)]
+
+    def head_part(k):
+        return gz32[link.zs[k]]
+
+    first = reduce_z_start(link, head_part, gz_sent, gz_got, 80)
     wait_all(got_b)
     bz[0] = by[0] + by[1] + by[2] + by[3]
-    got_b = [link.send(bz.at[0], bz.at[k], link.at(dz=k)) for k in range(1, NZ)]
-
-    wait_all(got_b)
+    interleave(gather_z(link, bz, None, lambda k: None))
+    got_z = reduce_z_finish(link, head_part, gz_sent, gz_got, 80, first)
     bias_sum = bz[0]
     for k in range(1, NZ):
         bias_sum = bias_sum + bz[k]
     bs[0] = bias_sum
     got_b = link.send(bs.at[0], bs.at[1], link.at(dc=1))
 
-    wait_all(got_z)
-    total = gz32[z]
-    for k in range(NZ - 1):
-        total = total + rz[k].astype(F32)
+    total = reduce_z_sum(head_part, gz_got, got_z)
     fin[0] = total[:, :36]
     fin[1] = total[:, 36:]
     got_w = link.send(fin.at[1 - c], ow.at[1], link.at(dc=1))
@@ -342,16 +461,25 @@
         ((2, NX - 1, ROWS, E), BF16),
         ((2, ROWS, E), F32),
         ((2, ROWS, 128), F32),
-        ((16, ROWS, E), BF16),
-        ((16, ROWS, E), BF16),
+        ((NX, NY, ROWS, E), BF16),
+        ((2, NZ, ROWS, E), BF16),
         ((512, 512), BF16),
         ((NZ, ROWS, E), F32),
         ((NZ, ROWS, E), F32),
         ((NZ, ROWS, E), F32),
-        ((2, NZ - 1, ROWS, E), BF16),
+        ((7, ROWS, E), BF16),
+        ((7, ROWS, E), BF16),
         ((ROWS, E), F32),
-        ((16, ROWS, E), BF16),
-        ((15, ROWS, E), BF16),
+        ((NX - 1, HALF, E), F32),
+        ((NY - 1, HALF, E), F32),
+        ((NY, NX, HALF, E), BF16),
+        ((NX, NY, HALF, E), BF16),
+        ((NY - 1, NX, HALF, E), BF16),
+        ((NX - 1, NY, HALF, E), BF16),
+        ((NX - 1, HALF, E), BF16),
+        ((NY - 1, HALF, E), BF16),
+        ((NX - 1, HALF, E), BF16),
+        ((NY - 1, HALF, E), BF16),
         ((2, ROWS, E), BF16),
         ((8, ROWS, E), BF16),
         ((24, 128), F32),
@@ -364,8 +492,8 @@
         ((NY, SHARD, E // 2), BF16),
         ((NY - 1, SHARD, E // 2), BF16),
         ((NZ, SHARD, 72), F32),
-        ((NZ, SHARD, 72), BF16),
-        ((NZ - 1, SHARD, 72), BF16),
+        ((7, SHARD, 72), BF16),
+        ((7, SHARD, 72), BF16),
         ((2, SHARD, 36), F32),
     ]
     parts = pl.pallas_call(

time: 112 us -> 102 us (0.911)
  Pallas kernels: 110 us -> 100 us
    pallas_call x1, Pallas kernels: 108 us -> 98.3 us  [per_device(): pl.pallas_call(kernel, out_shape=(jax.ShapeDtypeStruct((2, NX, ROWS, KX),...]
where the time goes in v3:
time: 102 us
  Pallas kernels  100 us (98%)
  between operations  1.93 us (2%)
    pallas_call x1, Pallas kernels, per_device(): pl.pallas_call(kernel, out_shape=(jax.ShapeDtypeStruct((2, NX, ROWS, KX),...  98.3 us

profile of v3, /device:TPU:1, one launch (start us, length us, event | category | flops | bytes accessed | tf_op | source)
XLA Modules:
  0.0 102.0 jit_solution(10351570753880633074)
XLA Ops:
  1.9 98.3 %shard_map.135 = (bf16[2,4,32,288]{3,2,1,0:T(8,128)(2,1)}, f32[2,144,36]{2,1,0:T(8,128)}, f32[24,128]{1,0:T(8,128)}) custom-call(bf16[32,1152]{1,0:T(8,128)(2,1)} %f_img.1, bf16[32,1152]{1,0:T(8,128)(2,1)} %f_txt.1, bf16[144,1152]{1,0:T(8,128)(2,1)} %w_img.1, bf16[144,1152]{1,0:T(8,128)(2,1)} %w_txt.1, f32[1152]{0:T(1024)} %b_img.1, f32[1152]{0:T(1024)} %b_txt.1, ...), custom_call_target="tpu_custom_call" | custom-call | tf_op jit(solution)/shard_map/pallas_call | solution.py:499
  100.2 1.8 %shard_map.136 = (f32[1]{0:T(128)}, f32[2]{0:T(128)}, bf16[32,1152]{1,0:T(8,128)(2,1)}, bf16[32,1152]{1,0:T(8,128)(2,1)}, f32[36,144]{1,0:T(8,128)}, /*index=5*/f32[36,144]{1,0:T(8,128)}, f32[2,1152]{1,0:T(2,128)}) custom-call(bf16[2,4,32,288]{3,2,1,0:T(8,128)(2,1)} %get-tuple-element.17.rf, f32[2,144,36]{2,1,0:T(8,128)} %get-tuple-element.18.ow, ...), custom_call_target="tpu_custom_call" | custom-call | tf_op jit(solution)/shard_map/pallas_call | solution.py:514

commit v4 on v3

--- a/solution.py
+++ b/solution.py
@@ -16,11 +16,14 @@
 E = 1152
 SHARD = 144
 KX = 2 * SHARD
+CHUNKS = 3
+COLS = E // CHUNKS
+CUT = SHARD // 3
 MESH = pl.DeviceIdType.MESH
 F32 = jnp.float32
 BF16 = jnp.bfloat16
 
-N_COPIES = 128
+N_GROUPS = 64
 
 
 def ring(place, size):
@@ -47,19 +50,40 @@
     def at(self, dx=0, dy=0, dz=0, dc=0):
         return (self.y_dp[dy] + self.z_dp[dz] + self.cs[dc], self.x_mp[dx] + self.y_mp[dy])
 
+    def group(self, region):
+        copies = Group(self, len(self.started), region)
+        self.started.append(copies)
+        return copies
+
     def send(self, src, dst, device):
-        k = len(self.started)
-        copy = pltpu.make_async_remote_copy(
+        copies = self.group(dst)
+        copies.send(src, dst, device)
+        return copies
+
+
+class Group:
+    def __init__(self, link, k, region):
+        self.link, self.region = link, region
+        self.sems = (link.send_sems.at[k], link.recv_sems.at[k])
+
+    def copy(self, src, dst, device):
+        return pltpu.make_async_remote_copy(
             src_ref=src,
             dst_ref=dst,
-            send_sem=self.send_sems.at[k],
-            recv_sem=self.recv_sems.at[k],
+            send_sem=self.sems[0],
+            recv_sem=self.sems[1],
             device_id=device,
             device_id_type=MESH,
         )
-        copy.start()
-        self.started.append(copy)
-        return copy
+
+    def send(self, src, dst, device):
+        self.copy(src, dst, device).start()
+
+    def wait_recv(self):
+        self.copy(self.region, self.region, self.link.at(dc=1)).wait_recv()
+
+    def wait_send(self):
+        self.copy(self.region, self.region, self.link.at(dc=1)).wait_send()
 
 
 def matmul(a, b):
@@ -116,7 +140,7 @@
 def gather_plane(link, buf):
     steps = (1, 3, 2)
     top, low = pl.ds(0, HALF), pl.ds(HALF, HALF)
-    got = []
+    got = link.group(buf.at[1:, 1:])
     got_x = [link.send(buf.at[0, 0], buf.at[NX - i, 0], link.at(dx=i)) for i in steps]
     got_y = [link.send(buf.at[0, 0], buf.at[0, NY - j], link.at(dy=j)) for j in steps]
     yield
@@ -124,12 +148,12 @@
         a = NX - k
         copy_x.wait_recv()
         for j in steps:
-            got.append(link.send(buf.at[a, 0, top], buf.at[a, NY - j, top], link.at(dy=j)))
+            got.send(buf.at[a, 0, top], buf.at[a, NY - j, top], link.at(dy=j))
         copy_y.wait_recv()
         for i in steps:
-            got.append(link.send(buf.at[0, a, low], buf.at[NX - i, a, low], link.at(dx=i)))
+            got.send(buf.at[0, a, low], buf.at[NX - i, a, low], link.at(dx=i))
         yield
-    wait_all(got)
+    got.wait_recv()
 
 
 def interleave(*parts):
@@ -153,23 +177,31 @@
     ]
 
 
-def reduce_z_finish(link, part, sent, got, split, first):
+def reduce_z_finish(link, part, sent, got, split, first, over_cores=False):
+    def onward(i, k):
+        if not over_cores:
+            return link.send(sent.at[i], got.at[i], link.at(dz=k))
+        copies = link.group(got.at[i])
+        for e in range(2):
+            copies.send(sent.at[i, link.cs[e]], got.at[i, e], link.at(dz=k, dc=e))
+        return copies
+
     first[0].wait_recv()
     sent[3] = (part(1) + got[0].astype(F32)).astype(BF16)
-    last = [link.send(sent.at[3], got.at[3], link.at(dz=1))]
+    last = [onward(3, 1)]
     first[1].wait_recv()
     sent[4] = (part(7) + got[1].astype(F32)).astype(BF16)
-    last.append(link.send(sent.at[4], got.at[4], link.at(dz=7)))
+    last.append(onward(4, 7))
     first[2].wait_recv()
     term = part(2)
     sent[5, :split] = (term[:split] + got[2, :split].astype(F32)).astype(BF16)
     sent[5, split:] = term[split:].astype(BF16)
-    last.append(link.send(sent.at[5], got.at[5], link.at(dz=2)))
+    last.append(onward(5, 2))
     first[3].wait_recv()
     term = part(6)
     sent[6, :split] = term[:split].astype(BF16)
     sent[6, split:] = (term[split:] + got[2, split:].astype(F32)).astype(BF16)
-    last.append(link.send(sent.at[6], got.at[6], link.at(dz=6)))
+    last.append(onward(6, 6))
     return last
 
 
@@ -186,7 +218,7 @@
     rf, ow, o_sums,
     fs, fk, wk, po, pk, rp0, rp, unit, inv, ia, ta, wt, tg, tgx, tgs, tz_sent, tz_got,
     ig0, ig_x32, ig_y32, ig_top, ig_low, r_top, r_low, ig2_top, ig2_low, r2_top, r2_low,
-    d16, dk, bp, bx, by, bz, bs, dfs, g32, gy, ry, gz32, gz_sent, gz_got, fin,
+    d16, dk, bp, bx, by, bz, bs, dfs, g32, gy, ry, gz32, gz_sent, gz_got, gz_own,
     send_sems, recv_sems,
 ):
     link = Links(send_sems, recv_sems)
@@ -195,20 +227,19 @@
     peers = [(0, 0, 0, 1)]
     peers += [(i, 0, 0, e) for i in range(1, NX) for e in range(2)]
     peers += [(0, j, 0, 0) for j in range(1, NY)]
-    peers += [(0, 0, k, 0) for k in (1, 2, 6, 7)]
+    peers += [(0, 0, k, e) for k in (1, 2, 6, 7) for e in range(2)]
     barrier = pltpu.get_barrier_semaphore()
     for p in peers:
         pl.semaphore_signal(barrier, inc=1, device_id=link.at(*p), device_id_type=MESH)
 
     shard = link.y_mp[0]
 
-    @pl.when(c == 0)
-    def _():
-        wk[shard] = w_img[...]
-
-    @pl.when(c == 1)
-    def _():
-        wk[shard] = w_txt[...]
+    for t, head in enumerate((w_img, w_txt)):
+
+        @pl.when(c == t)
+        def _():
+            for k in range(CHUNKS):
+                wk[k, shard] = head[:, COLS * k : COLS * (k + 1)]
 
     for k in range(NX):
         fs[0, k] = f_img[:, KX * k : KX * (k + 1)]
@@ -218,49 +249,56 @@
     odd = y - 2 * shard
     ahead, behind = link.at(dy=1), link.at(dy=3)
     partner = tuple(jnp.where(odd == 1, u, v) for u, v in zip(ahead, behind))
-    got_w = link.send(wk.at[shard], wk.at[shard], partner)
-    got_f = []
+    got_f = link.group(fk.at[1:])
     for r in range(NX):
         for e in range(2):
             if (r, e) == (0, 0):
                 fk[0] = fs[c, x]
                 continue
-            got_f.append(
-                link.send(
-                    fs.at[link.cs[e], link.xs[r]],
-                    fk.at[((NX - r) % NX) * 2 + e],
-                    link.at(dx=r, dc=e),
-                )
+            got_f.send(
+                fs.at[link.cs[e], link.xs[r]],
+                fk.at[((NX - r) % NX) * 2 + e],
+                link.at(dx=r, dc=e),
             )
-    wait_all(got_f)
-    got_w.wait_recv()
-
-    part = matmul(fk[...].reshape(8 * ROWS, KX), wk[...].reshape(KX, E))
-    rp0[0] = part[:ROWS]
-    po[...] = part[ROWS : 2 * ROWS]
-    pk[...] = part[2 * ROWS :].astype(BF16).reshape(6, ROWS, E)
-    got_p = [link.send(po, rp0.at[1], link.at(dc=1))]
-    for r in range(1, NX):
-        for e in range(2):
-            got_p.append(
-                link.send(pk.at[(r - 1) * 2 + e], rp.at[e, NX - r - 1], link.at(dx=r, dc=e))
-            )
-    wait_all(got_p)
-    for t, bias in enumerate((b_img, b_txt)):
-        e = link.cs[t]
-        pre = rp0[e] + bias[...].reshape(1, E)
-        for r in range(NX - 1):
-            pre = pre + rp[e, r].astype(F32)
-        inverse = lax.rsqrt(jnp.sum(pre * pre, axis=1, keepdims=True) + EPSILON)
-        unit[t] = pre * inverse
+    got_w = [link.send(wk.at[k, shard], wk.at[k, shard], partner) for k in range(CHUNKS)]
+    got_f.wait_recv()
+
+    rows = fk[...].reshape(8 * ROWS, KX)
+    got_p = []
+    for k in range(CHUNKS):
+        got_w[k].wait_recv()
+        part = matmul(rows, wk[k].reshape(KX, COLS))
+        rp0[k, 0] = part[:ROWS]
+        po[k] = part[ROWS : 2 * ROWS]
+        pk[k] = part[2 * ROWS :].astype(BF16).reshape(6, ROWS, COLS)
+        got = link.group(rp.at[k])
+        got_p.append([link.send(po.at[k], rp0.at[k, 1], link.at(dc=1)), got])
+        for r in (2, 1, 3):
+            for e in range(2):
+                got.send(pk.at[k, (r - 1) * 2 + e], rp.at[k, e, NX - r - 1], link.at(dx=r, dc=e))
+    squares = [0.0, 0.0]
+    for k in range(CHUNKS):
+        wait_all(got_p[k])
+        cols = slice(COLS * k, COLS * (k + 1))
+        for t, bias in enumerate((b_img, b_txt)):
+            e = link.cs[t]
+            pre = rp0[k, e] + bias[cols].reshape(1, COLS)
+            for r in range(NX - 1):
+                pre = pre + rp[k, e, r].astype(F32)
+            unit[t, :, cols] = pre
+            squares[t] = squares[t] + jnp.sum(pre * pre, axis=1, keepdims=True)
+    for t in range(2):
+        inverse = lax.rsqrt(squares[t] + EPSILON)
+        unit[t] = unit[t] * inverse
         inv[t] = jnp.broadcast_to(inverse, (ROWS, 128))
     ia[0, 0] = unit[0].astype(BF16)
     ta[0, 0] = unit[1].astype(BF16)
 
-    got_s = [link.send(ta.at[0, 0], ta.at[1, 0], link.at(dc=1))]
+    got_s = link.group(ta.at[1])
+    got_s.send(ta.at[0, 0], ta.at[1, 0], link.at(dc=1))
 
     def forward(k):
-        got_s.append(link.send(ta.at[0, k], ta.at[1, k], link.at(dc=1)))
+        got_s.send(ta.at[0, k], ta.at[1, k], link.at(dc=1))
 
     interleave(gather_z(link, ta.at[0], HALF, forward), gather_plane(link, ia))
 
@@ -271,7 +309,7 @@
     stats = []
     for h in range(2):
         if h == 1:
-            wait_all(got_s)
+            got_s.wait_recv()
         texts = ta[h].reshape(half, E)
         scaled = scale * matmul_bt(texts, images)
         logits = scaled + shift
@@ -305,14 +343,14 @@
 
     top, low = pl.ds(0, HALF), pl.ds(HALF, HALF)
     texts = ta[...].reshape(16 * ROWS, E)
-    got_low, got_top = [], []
+    got_low, got_top = link.group(r_low), link.group(r_top)
     for i, a in enumerate((2, 1, 3, 0)):
         grad = matmul(wt[128 * a : 128 * (a + 1), :], texts).reshape(NY, ROWS, E)
         ig_top[:, a] = grad[:, :HALF].astype(BF16)
         ig_low[a] = grad[:, HALF:].astype(BF16)
         if a:
             ig_x32[a - 1] = grad[0, :HALF]
-            got_low.append(link.send(ig_low.at[a], r_low.at[a - 1], link.at(dx=a)))
+            got_low.send(ig_low.at[a], r_low.at[a - 1], link.at(dx=a))
         else:
             ig0[...] = grad[0]
             ig_y32[...] = grad[1:, HALF:]
@@ -320,29 +358,30 @@
             got_x[0].wait_recv()
             first = reduce_z_start(link, txt_part, tz_sent, tz_got, HALF)
     for j in (2, 1, 3):
-        got_top.append(link.send(ig_top.at[j], r_top.at[j - 1], link.at(dy=j)))
+        got_top.send(ig_top.at[j], r_top.at[j - 1], link.at(dy=j))
     wait_all(got_x[1:])
     got_tg = reduce_z_finish(link, txt_part, tz_sent, tz_got, HALF, first)
 
-    wait_all(got_low)
-    got_low2 = []
+    got_low.wait_recv()
+    got_low2 = link.group(r2_low)
     for j in (2, 1, 3):
         total = ig_y32[j - 1]
         for i in range(NX - 1):
             total = total + r_low[i, j].astype(F32)
         ig2_low[j - 1] = total.astype(BF16)
-        got_low2.append(link.send(ig2_low.at[j - 1], r2_low.at[j - 1], link.at(dy=j)))
-    wait_all(got_top)
-    got_top2 = []
+        got_low2.send(ig2_low.at[j - 1], r2_low.at[j - 1], link.at(dy=j))
+    got_top.wait_recv()
+    got_top2 = link.group(r2_top)
     for i in (2, 1, 3):
         total = ig_x32[i - 1]
         for j in range(NY - 1):
             total = total + r_top[j, i].astype(F32)
         ig2_top[i - 1] = total.astype(BF16)
-        got_top2.append(link.send(ig2_top.at[i - 1], r2_top.at[i - 1], link.at(dx=i)))
+        got_top2.send(ig2_top.at[i - 1], r2_top.at[i - 1], link.at(dx=i))
 
     grad_txt = reduce_z_sum(txt_part, tz_got, got_tg)
-    wait_all(got_low2 + got_top2)
+    got_low2.wait_recv()
+    got_top2.wait_recv()
     halves = []
     for rows, first_got, second_got in ((top, r_top, r2_top), (low, r_low, r2_low)):
         total = ig0[rows, :]
@@ -364,19 +403,22 @@
         )
     bp[21:24, :] = jnp.zeros((3, 128), F32)
 
-    got_d = []
+    got_b = link.group(bx)
+    for r in range(1, NX):
+        got_b.send(bp, bx.at[r - 1], link.at(dx=r))
+    got_d = link.group(dk.at[1:])
     for r in range(NX):
         for e in range(2):
             if (r, e) == (0, 0):
                 dk[0] = d16[c]
                 continue
-            got_d.append(
-                link.send(
-                    d16.at[link.cs[e]], dk.at[((NX - r) % NX) * 2 + e], link.at(dx=r, dc=e)
-                )
-            )
-    got_b = [link.send(bp, bx.at[r - 1], link.at(dx=r)) for r in range(1, NX)]
-    wait_all(got_d)
+            got_d.send(d16.at[link.cs[e]], dk.at[((NX - r) % NX) * 2 + e], link.at(dx=r, dc=e))
+    got_b.wait_recv()
+    by[0] = bp[...] + bx[0] + bx[1] + bx[2]
+    got_b = link.group(by.at[1:])
+    for j in range(1, NY):
+        got_b.send(by.at[0], by.at[j], link.at(dy=j))
+    got_d.wait_recv()
 
     deltas = dk[...].reshape(8 * ROWS, E)
     grad_w = matmul_at(fk[...].reshape(8 * ROWS, KX), deltas)
@@ -384,51 +426,56 @@
         part = grad_w[SHARD * (j // 2) : SHARD * (j // 2 + 1), (E // 2) * (j % 2) : (E // 2) * (j % 2 + 1)]
         g32[j] = part
         gy[j] = part.astype(BF16)
-    got_y = [link.send(gy.at[link.ys[j]], ry.at[j - 1], link.at(dy=j)) for j in (2, 1, 3)]
-    wait_all(got_b)
-    by[0] = bp[...] + bx[0] + bx[1] + bx[2]
-    got_b = [link.send(by.at[0], by.at[j], link.at(dy=j)) for j in range(1, NY)]
-
-    grad_f = matmul_bt(deltas, wk[...].reshape(KX, E)).astype(BF16)
-    dfs[...] = grad_f.reshape(8, ROWS, KX)
-    got_df = []
+    got_y = link.group(ry)
+    for j in (2, 1, 3):
+        got_y.send(gy.at[link.ys[j]], ry.at[j - 1], link.at(dy=j))
+
+    grad_f = 0.0
+    for k in range(CHUNKS):
+        grad_f = grad_f + matmul_bt(deltas[:, COLS * k : COLS * (k + 1)], wk[k].reshape(KX, COLS))
+    dfs[...] = grad_f.astype(BF16).reshape(8, ROWS, KX)
+    got_df = link.group(dfs.at[1:])
     for r in range(NX):
         for e in range(2):
             if (r, e) == (0, 0):
                 rf[0, x] = dfs[0]
                 continue
-            got_df.append(link.send(dfs.at[r * 2 + e], rf.at[e, x], link.at(dx=r, dc=e)))
-
-    wait_all(got_y)
-    total = g32[y]
-    for j in range(NY - 1):
-        total = total + ry[j].astype(F32)
-    for k in range(NZ):
-        gz32[k] = total[:, 72 * k : 72 * (k + 1)]
-
-    def head_part(k):
-        return gz32[link.zs[k]]
-
-    first = reduce_z_start(link, head_part, gz_sent, gz_got, 80)
-    wait_all(got_b)
+            got_df.send(dfs.at[r * 2 + e], rf.at[e, x], link.at(dx=r, dc=e))
+
+    got_b.wait_recv()
     bz[0] = by[0] + by[1] + by[2] + by[3]
     interleave(gather_z(link, bz, None, lambda k: None))
-    got_z = reduce_z_finish(link, head_part, gz_sent, gz_got, 80, first)
     bias_sum = bz[0]
     for k in range(1, NZ):
         bias_sum = bias_sum + bz[k]
     bs[0] = bias_sum
     got_b = link.send(bs.at[0], bs.at[1], link.at(dc=1))
 
-    total = reduce_z_sum(head_part, gz_got, got_z)
-    fin[0] = total[:, :36]
-    fin[1] = total[:, 36:]
-    got_w = link.send(fin.at[1 - c], ow.at[1], link.at(dc=1))
+    got_y.wait_recv()
+    total = g32[y]
+    for j in range(NY - 1):
+        total = total + ry[j].astype(F32)
+    for k in range(NZ):
+        for e in range(2):
+            col = 72 * k + 36 * e
+            block = total[:, col : col + 36]
+            gz32[k, e] = jnp.concatenate([block[:CUT], block[CUT : 2 * CUT], block[2 * CUT :]], axis=1)
+
+    def head_part(k):
+        return gz32[link.zs[k]]
+
+    first = reduce_z_start(link, head_part, gz_sent, gz_got, 1)
+    got_own = link.send(gz32.at[z, link.cs[1]], gz_own, link.at(dc=1))
+    last = reduce_z_finish(link, head_part, gz_sent, gz_got, 1, first, over_cores=True)
+    got_own.wait_recv()
+    wait_all(last)
+    for e, total in enumerate((gz32[z, c], gz_own[...])):
+        for i in range(4):
+            total = total + gz_got[3 + i, e].astype(F32)
+        ow[e] = total
     got_b.wait_recv()
     o_sums[...] = bs[0] + bs[1]
-    got_w.wait_recv()
-    ow[0] = fin[c]
-    wait_all(got_df)
+    got_df.wait_recv()
 
     for copy in link.started:
         copy.wait_send()
@@ -440,7 +487,8 @@
         e = jnp.where(c == t, 0, 1)
         for k in range(NX):
             out_f[:, KX * k : KX * (k + 1)] = rf[e, k]
-        out_w[...] = ow[e].T
+        for k in range(3):
+            out_w[:, CUT * k : CUT * (k + 1)] = ow[e][:, 36 * k : 36 * (k + 1)].T
         for k in range(9):
             o_bias[t : t + 1, 128 * k : 128 * (k + 1)] = sums[9 * t + k : 9 * t + k + 1, :]
     o_loss[0] = jnp.sum(sums[18:19, :]) * (1.0 / 8192.0)
@@ -454,11 +502,11 @@
     scratch = [
         ((2, NX, ROWS, KX), BF16),
         ((8, ROWS, KX), BF16),
-        ((2, SHARD, E), BF16),
-        ((ROWS, E), F32),
-        ((6, ROWS, E), BF16),
-        ((2, ROWS, E), F32),
-        ((2, NX - 1, ROWS, E), BF16),
+        ((CHUNKS, 2, SHARD, COLS), BF16),
+        ((CHUNKS, ROWS, COLS), F32),
+        ((CHUNKS, 6, ROWS, COLS), BF16),
+        ((CHUNKS, 2, ROWS, COLS), F32),
+        ((CHUNKS, 2, NX - 1, ROWS, COLS), BF16),
         ((2, ROWS, E), F32),
         ((2, ROWS, 128), F32),
         ((NX, NY, ROWS, E), BF16),
@@ -491,22 +539,22 @@
         ((NY, SHARD, E // 2), F32),
         ((NY, SHARD, E // 2), BF16),
         ((NY - 1, SHARD, E // 2), BF16),
-        ((NZ, SHARD, 72), F32),
-        ((7, SHARD, 72), BF16),
-        ((7, SHARD, 72), BF16),
-        ((2, SHARD, 36), F32),
+        ((NZ, 2, CUT, 108), F32),
+        ((7, 2, CUT, 108), BF16),
+        ((7, 2, CUT, 108), BF16),
+        ((CUT, 108), F32),
     ]
     parts = pl.pallas_call(
         kernel,
         out_shape=(
             jax.ShapeDtypeStruct((2, NX, ROWS, KX), BF16),
-            jax.ShapeDtypeStruct((2, SHARD, 36), F32),
+            jax.ShapeDtypeStruct((2, CUT, 108), F32),
             jax.ShapeDtypeStruct((24, 128), F32),
         ),
         in_specs=[vmem] * 8,
         out_specs=(vmem, vmem, vmem),
         scratch_shapes=[pltpu.VMEM(shape, dtype) for shape, dtype in scratch]
-        + [pltpu.SemaphoreType.DMA((N_COPIES,))] * 2,
+        + [pltpu.SemaphoreType.DMA((N_GROUPS,))] * 2,
         compiler_params=pltpu.CompilerParams(
             collective_id=0, has_side_effects=True, vmem_limit_bytes=56 * 2**20
         ),

time: 102 us -> 90 us (0.88)
  Pallas kernels: 100 us -> 88 us
    pallas_call x1, Pallas kernels: 98.3 us -> 85.9 us  [per_device(): pl.pallas_call(kernel, out_shape=(jax.ShapeDtypeStruct((2, NX, ROWS, KX),...]
where the time goes in v4:
time: 90 us; the launch traced here: 89.9 us
  Pallas kernels  88 us (98%)
  between operations  1.93 us (2%)
    pallas_call x1, Pallas kernels, per_device(): pl.pallas_call(kernel, out_shape=(jax.ShapeDtypeStruct((2, NX, ROWS, KX),...  85.9 us
    pallas_call x1, Pallas kernels, per_device(): pl.pallas_call(finish, out_shape=(jax.ShapeDtypeStruct((1,), F32), jax.Sh...  2.02 us

profile of v4, /device:TPU:1, one launch (start us, length us, event | category | flops | bytes accessed | tf_op | source)
XLA Modules:
  0.0 89.9 jit_solution(7667535070200241791)
XLA Ops:
  1.9 85.9 %shard_map.135 = (bf16[2,4,32,288]{3,2,1,0:T(8,128)(2,1)}, f32[2,48,108]{2,1,0:T(8,128)}, f32[24,128]{1,0:T(8,128)}) custom-call(bf16[32,1152]{1,0:T(8,128)(2,1)} %f_img.1, bf16[32,1152]{1,0:T(8,128)(2,1)} %f_txt.1, bf16[144,1152]{1,0:T(8,128)(2,1)} %w_img.1, bf16[144,1152]{1,0:T(8,128)(2,1)} %w_txt.1, f32[1152]{0:T(1024)} %b_img.1, f32[1152]{0:T(1024)} %b_txt.1, ...), custom_call_target="tpu_custom_call" | custom-call | tf_op jit(solution)/shard_map/pallas_call | solution.py:547
  87.9 2.0 %shard_map.136 = (f32[1]{0:T(128)}, f32[2]{0:T(128)}, bf16[32,1152]{1,0:T(8,128)(2,1)}, bf16[32,1152]{1,0:T(8,128)(2,1)}, f32[36,144]{1,0:T(8,128)}, /*index=5*/f32[36,144]{1,0:T(8,128)}, f32[2,1152]{1,0:T(2,128)}) custom-call(bf16[2,4,32,288]{3,2,1,0:T(8,128)(2,1)} %get-tuple-element.17.rf, f32[2,48,108]{2,1,0:T(8,128)} %get-tuple-element.18.ow, ...), custom_call_target="tpu_custom_call" | custom-call | tf_op jit(solution)/shard_map/pallas_call | solution.py:562

commit v5 on v4

--- a/solution.py
+++ b/solution.py
@@ -19,11 +19,12 @@
 CHUNKS = 3
 COLS = E // CHUNKS
 CUT = SHARD // 3
+QUARTER = E // 4
 MESH = pl.DeviceIdType.MESH
 F32 = jnp.float32
 BF16 = jnp.bfloat16
 
-N_GROUPS = 64
+N_GROUPS = 65
 
 
 def ring(place, size):
@@ -216,7 +217,7 @@
 def kernel(
     f_img, f_txt, w_img, w_txt, b_img, b_txt, log_scale, logit_bias,
     rf, ow, o_sums,
-    fs, fk, wk, po, pk, rp0, rp, unit, inv, ia, ta, wt, tg, tgx, tgs, tz_sent, tz_got,
+    fs, fk, wk, po, pk, rp0, rp, unit, inv, ia, ta, wt, wn, tg, tgx, tgs, tz_sent, tz_got,
     ig0, ig_x32, ig_y32, ig_top, ig_low, r_top, r_low, ig2_top, ig2_low, r2_top, r2_low,
     d16, dk, bp, bx, by, bz, bs, dfs, g32, gy, ry, gz32, gz_sent, gz_got, gz_own,
     send_sems, recv_sems,
@@ -328,11 +329,9 @@
         sums = (loss, LOSS_FACTOR * errors * scaled, LOSS_FACTOR * errors)
         stats.append([jnp.sum(v, axis=0, keepdims=True) for v in sums])
         wt[:, half * h : half * (h + 1)] = weights.T
-        grad = matmul(weights, images)
         if h == 0:
-            tg[...] = grad.reshape(NZ, ROWS, E)
-        else:
-            tgx[...] = grad.reshape(NZ, ROWS, E)
+            wn[...] = weights
+    tgx[...] = matmul(weights, images).reshape(NZ, ROWS, E)
     got_x = [
         link.send(tgx.at[k], tgs.at[k], link.at(dc=1))
         for k in (pl.ds(3, 3), pl.ds(0, 3), pl.ds(6, 2))
@@ -355,6 +354,7 @@
             ig0[...] = grad[0]
             ig_y32[...] = grad[1:, HALF:]
         if i == 0:
+            tg[...] = matmul(wn[...], images).reshape(NZ, ROWS, E)
             got_x[0].wait_recv()
             first = reduce_z_start(link, txt_part, tz_sent, tz_got, HALF)
     for j in (2, 1, 3):
@@ -392,7 +392,10 @@
     for t, grad in enumerate((grad_img, grad_txt)):
         grad = scale * grad
         delta = inv[t, :, 0:1] * (grad - unit[t] * jnp.sum(unit[t] * grad, axis=1, keepdims=True))
-        d16[t] = delta.astype(BF16)
+        for h in range(2):
+            for q in range(2):
+                col = 2 * QUARTER * q + QUARTER * h
+                d16[h, t, :, QUARTER * q : QUARTER * (q + 1)] = delta[:, col : col + QUARTER].astype(BF16)
         total = jnp.sum(delta, axis=0, keepdims=True)
         for k in range(9):
             bp[9 * t + k : 9 * t + k + 1, :] = total[:, 128 * k : 128 * (k + 1)]
@@ -406,30 +409,40 @@
     got_b = link.group(bx)
     for r in range(1, NX):
         got_b.send(bp, bx.at[r - 1], link.at(dx=r))
-    got_d = link.group(dk.at[1:])
-    for r in range(NX):
-        for e in range(2):
-            if (r, e) == (0, 0):
-                dk[0] = d16[c]
-                continue
-            got_d.send(d16.at[link.cs[e]], dk.at[((NX - r) % NX) * 2 + e], link.at(dx=r, dc=e))
+    got_d = []
+    for h in range(2):
+        got_d.append(link.group(dk.at[h, 1:]))
+        for r in (0, 2, 1, 3):
+            for e in range(2):
+                if (r, e) == (0, 0):
+                    dk[h, 0] = d16[h, c]
+                    continue
+                got_d[h].send(
+                    d16.at[h, link.cs[e]], dk.at[h, ((NX - r) % NX) * 2 + e], link.at(dx=r, dc=e)
+                )
     got_b.wait_recv()
     by[0] = bp[...] + bx[0] + bx[1] + bx[2]
     got_b = link.group(by.at[1:])
     for j in range(1, NY):
         got_b.send(by.at[0], by.at[j], link.at(dy=j))
-    got_d.wait_recv()
-
-    deltas = dk[...].reshape(8 * ROWS, E)
-    grad_w = matmul_at(fk[...].reshape(8 * ROWS, KX), deltas)
-    for j in range(NY):
-        part = grad_w[SHARD * (j // 2) : SHARD * (j // 2 + 1), (E // 2) * (j % 2) : (E // 2) * (j % 2 + 1)]
-        g32[j] = part
-        gy[j] = part.astype(BF16)
-    got_y = link.group(ry)
-    for j in (2, 1, 3):
-        got_y.send(gy.at[link.ys[j]], ry.at[j - 1], link.at(dy=j))
-
+
+    rows = fk[...].reshape(8 * ROWS, KX)
+    got_y, deltas = [], []
+    for h in range(2):
+        got_d[h].wait_recv()
+        half_deltas = dk[h].reshape(8 * ROWS, 2 * QUARTER)
+        deltas.append(half_deltas)
+        grad_w = matmul_at(rows, half_deltas)
+        for j in range(NY):
+            block = grad_w[SHARD * (j // 2) : SHARD * (j // 2 + 1), QUARTER * (j % 2) : QUARTER * (j % 2 + 1)]
+            block = jnp.concatenate([block[:CUT], block[CUT : 2 * CUT], block[2 * CUT :]], axis=1)
+            g32[h, j] = block
+            gy[h, j] = block.astype(BF16)
+        got_y.append(link.group(ry.at[h]))
+        for j in (2, 1, 3):
+            got_y[h].send(gy.at[h, link.ys[j]], ry.at[h, j - 1], link.at(dy=j))
+
+    deltas = jnp.concatenate([d[:, QUARTER * q : QUARTER * (q + 1)] for q in range(2) for d in deltas], axis=1)
     grad_f = 0.0
     for k in range(CHUNKS):
         grad_f = grad_f + matmul_bt(deltas[:, COLS * k : COLS * (k + 1)], wk[k].reshape(KX, COLS))
@@ -451,15 +464,16 @@
     bs[0] = bias_sum
     got_b = link.send(bs.at[0], bs.at[1], link.at(dc=1))
 
-    got_y.wait_recv()
-    total = g32[y]
-    for j in range(NY - 1):
-        total = total + ry[j].astype(F32)
-    for k in range(NZ):
-        for e in range(2):
-            col = 72 * k + 36 * e
-            block = total[:, col : col + 36]
-            gz32[k, e] = jnp.concatenate([block[:CUT], block[CUT : 2 * CUT], block[2 * CUT :]], axis=1)
+    for h in range(2):
+        got_y[h].wait_recv()
+        total = g32[h, y]
+        for j in range(NY - 1):
+            total = total + ry[h, j].astype(F32)
+        for k in range(NZ // 2):
+            for e in range(2):
+                col = 72 * k + 36 * e
+                block = [total[:, QUARTER * i + col : QUARTER * i + col + 36] for i in range(3)]
+                gz32[NZ // 2 * h + k, e] = jnp.concatenate(block, axis=1)
 
     def head_part(k):
         return gz32[link.zs[k]]
@@ -512,6 +526,7 @@
         ((NX, NY, ROWS, E), BF16),
         ((2, NZ, ROWS, E), BF16),
         ((512, 512), BF16),
+        ((256, 512), BF16),
         ((NZ, ROWS, E), F32),
         ((NZ, ROWS, E), F32),
         ((NZ, ROWS, E), F32),
@@ -528,17 +543,17 @@
         ((NY - 1, HALF, E), BF16),
         ((NX - 1, HALF, E), BF16),
         ((NY - 1, HALF, E), BF16),
-        ((2, ROWS, E), BF16),
-        ((8, ROWS, E), BF16),
+        ((2, 2, ROWS, 2 * QUARTER), BF16),
+        ((2, 8, ROWS, 2 * QUARTER), BF16),
         ((24, 128), F32),
         ((3, 24, 128), F32),
         ((4, 24, 128), F32),
         ((8, 24, 128), F32),
         ((2, 24, 128), F32),
         ((8, ROWS, KX), BF16),
-        ((NY, SHARD, E // 2), F32),
-        ((NY, SHARD, E // 2), BF16),
-        ((NY - 1, SHARD, E // 2), BF16),
+        ((2, NY, CUT, 3 * QUARTER), F32),
+        ((2, NY, CUT, 3 * QUARTER), BF16),
+        ((2, NY - 1, CUT, 3 * QUARTER), BF16),
         ((NZ, 2, CUT, 108), F32),
         ((7, 2, CUT, 108), BF16),
         ((7, 2, CUT, 108), BF16),

time: 90 us -> 88.3 us (0.981)
  Pallas kernels: 88 us -> 86.2 us
    pallas_call x1, Pallas kernels: 85.9 us -> 84.2 us  [per_device(): pl.pallas_call(kernel, out_shape=(jax.ShapeDtypeStruct((2, NX, ROWS, KX),...]
where the time goes in v5:
time: 88.3 us; the launch traced here: 88.1 us
  Pallas kernels  86.2 us (98%)
  between operations  1.93 us (2%)
    pallas_call x1, Pallas kernels, per_device(): pl.pallas_call(kernel, out_shape=(jax.ShapeDtypeStruct((2, NX, ROWS, KX),...  84.2 us
    pallas_call x1, Pallas kernels, per_device(): pl.pallas_call(finish, out_shape=(jax.ShapeDtypeStruct((1,), F32), jax.Sh...  2.02 us

profile of v5, /device:TPU:1, one launch (start us, length us, event | category | flops | bytes accessed | tf_op | source)
XLA Modules:
  0.0 88.1 jit_solution(2356983431473534806)
XLA Ops:
  1.9 84.2 %shard_map.135 = (bf16[2,4,32,288]{3,2,1,0:T(8,128)(2,1)}, f32[2,48,108]{2,1,0:T(8,128)}, f32[24,128]{1,0:T(8,128)}) custom-call(bf16[32,1152]{1,0:T(8,128)(2,1)} %f_img.1, bf16[32,1152]{1,0:T(8,128)(2,1)} %f_txt.1, bf16[144,1152]{1,0:T(8,128)(2,1)} %w_img.1, bf16[144,1152]{1,0:T(8,128)(2,1)} %w_txt.1, f32[1152]{0:T(1024)} %b_img.1, f32[1152]{0:T(1024)} %b_txt.1, ...), custom_call_target="tpu_custom_call" | custom-call | tf_op jit(solution)/shard_map/pallas_call | solution.py:562
  86.1 2.0 %shard_map.136 = (f32[1]{0:T(128)}, f32[2]{0:T(128)}, bf16[32,1152]{1,0:T(8,128)(2,1)}, bf16[32,1152]{1,0:T(8,128)(2,1)}, f32[36,144]{1,0:T(8,128)}, /*index=5*/f32[36,144]{1,0:T(8,128)}, f32[2,1152]{1,0:T(2,128)}) custom-call(bf16[2,4,32,288]{3,2,1,0:T(8,128)(2,1)} %get-tuple-element.17.rf, f32[2,48,108]{2,1,0:T(8,128)} %get-tuple-element.18.ow, ...), custom_call_target="tpu_custom_call" | custom-call | tf_op jit(solution)/shard_map/pallas_call | solution.py:577

commit v6 on v5

--- a/solution.py
+++ b/solution.py
@@ -105,20 +105,13 @@
 
 
 def gather_z(link, buf, split, on_arrival):
+    to_6 = link.send(buf.at[0], buf.at[6], link.at(dz=2))
+    to_2 = link.send(buf.at[0], buf.at[2], link.at(dz=6))
     to_7 = link.send(buf.at[0], buf.at[7], link.at(dz=1))
     to_1 = link.send(buf.at[0], buf.at[1], link.at(dz=7))
-    to_6 = link.send(buf.at[0], buf.at[6], link.at(dz=2))
-    to_2 = link.send(buf.at[0], buf.at[2], link.at(dz=6))
-    yield
-    to_7.wait_recv()
-    to_5 = link.send(buf.at[7], buf.at[5], link.at(dz=2))
-    on_arrival(7)
-    yield
-    to_1.wait_recv()
-    to_3 = link.send(buf.at[1], buf.at[3], link.at(dz=6))
-    on_arrival(1)
     yield
     to_6.wait_recv()
+    to_5 = link.send(buf.at[6], buf.at[5], link.at(dz=1))
     if split is None:
         to_4 = [link.send(buf.at[6], buf.at[4], link.at(dz=2))]
     else:
@@ -126,9 +119,16 @@
     on_arrival(6)
     yield
     to_2.wait_recv()
+    to_3 = link.send(buf.at[2], buf.at[3], link.at(dz=7))
     if split is not None:
         to_4.append(link.send(buf.at[2, split:], buf.at[4, split:], link.at(dz=6)))
     on_arrival(2)
+    yield
+    to_7.wait_recv()
+    on_arrival(7)
+    yield
+    to_1.wait_recv()
+    on_arrival(1)
     yield
     to_5.wait_recv()
     on_arrival(5)
@@ -168,13 +168,13 @@
 
 
 def reduce_z_start(link, part, sent, got, split):
-    for i, k in enumerate((3, 5, 4)):
+    for i, k in enumerate((4, 3, 5)):
         sent[i] = part(k).astype(BF16)
     return [
-        link.send(sent.at[0], got.at[0], link.at(dz=2)),
-        link.send(sent.at[1], got.at[1], link.at(dz=6)),
-        link.send(sent.at[2, :split], got.at[2, :split], link.at(dz=2)),
-        link.send(sent.at[2, split:], got.at[2, split:], link.at(dz=6)),
+        link.send(sent.at[0, :split], got.at[0, :split], link.at(dz=2)),
+        link.send(sent.at[0, split:], got.at[0, split:], link.at(dz=6)),
+        link.send(sent.at[1], got.at[1], link.at(dz=1)),
+        link.send(sent.at[2], got.at[2], link.at(dz=7)),
     ]
 
 
@@ -187,21 +187,21 @@
             copies.send(sent.at[i, link.cs[e]], got.at[i, e], link.at(dz=k, dc=e))
         return copies
 
+    last = []
+    for i, k in ((3, 1), (4, 7)):
+        sent[i] = part(k).astype(BF16)
+        last.append(onward(i, k))
     first[0].wait_recv()
-    sent[3] = (part(1) + got[0].astype(F32)).astype(BF16)
-    last = [onward(3, 1)]
-    first[1].wait_recv()
-    sent[4] = (part(7) + got[1].astype(F32)).astype(BF16)
-    last.append(onward(4, 7))
     first[2].wait_recv()
-    term = part(2)
-    sent[5, :split] = (term[:split] + got[2, :split].astype(F32)).astype(BF16)
+    term = part(2) + got[1].astype(F32)
+    sent[5, :split] = (term[:split] + got[0, :split].astype(F32)).astype(BF16)
     sent[5, split:] = term[split:].astype(BF16)
     last.append(onward(5, 2))
+    first[1].wait_recv()
     first[3].wait_recv()
-    term = part(6)
+    term = part(6) + got[2].astype(F32)
     sent[6, :split] = term[:split].astype(BF16)
-    sent[6, split:] = (term[split:] + got[2, split:].astype(F32)).astype(BF16)
+    sent[6, split:] = (term[split:] + got[0, split:].astype(F32)).astype(BF16)
     last.append(onward(6, 6))
     return last
 
@@ -217,13 +217,28 @@
 def kernel(
     f_img, f_txt, w_img, w_txt, b_img, b_txt, log_scale, logit_bias,
     rf, ow, o_sums,
-    fs, fk, wk, po, pk, rp0, rp, unit, inv, ia, ta, wt, wn, tg, tgx, tgs, tz_sent, tz_got,
+    fv, fs, fk, wk, po, pk, rp0, rp, unit, inv, ia, ta, wt, wn, tg, tgx, tgs, tz_sent, tz_got,
     ig0, ig_x32, ig_y32, ig_top, ig_low, r_top, r_low, ig2_top, ig2_low, r2_top, r2_low,
     d16, dk, bp, bx, by, bz, bs, dfs, g32, gy, ry, gz32, gz_sent, gz_got, gz_own,
-    send_sems, recv_sems,
+    send_sems, recv_sems, load_sems,
 ):
     link = Links(send_sems, recv_sems)
     x, y, z, c = link.x, link.y, link.z, link.c
+
+    shard = link.y_mp[0]
+    for t, head in enumerate((w_img, w_txt)):
+
+        @pl.when(c == t)
+        def _():
+            for k in range(CHUNKS):
+                cols = pl.ds(COLS * k, COLS)
+                pltpu.make_async_copy(head.at[:, cols], wk.at[k, shard], load_sems.at[0]).start()
+
+    loads = [
+        pltpu.make_async_copy(f, fv.at[t], load_sems.at[1 + t]) for t, f in enumerate((f_img, f_txt))
+    ]
+    for load in loads:
+        load.start()
 
     peers = [(0, 0, 0, 1)]
     peers += [(i, 0, 0, e) for i in range(1, NX) for e in range(2)]
@@ -233,18 +248,12 @@
     for p in peers:
         pl.semaphore_signal(barrier, inc=1, device_id=link.at(*p), device_id_type=MESH)
 
-    shard = link.y_mp[0]
-
-    for t, head in enumerate((w_img, w_txt)):
-
-        @pl.when(c == t)
-        def _():
-            for k in range(CHUNKS):
-                wk[k, shard] = head[:, COLS * k : COLS * (k + 1)]
-
-    for k in range(NX):
-        fs[0, k] = f_img[:, KX * k : KX * (k + 1)]
-        fs[1, k] = f_txt[:, KX * k : KX * (k + 1)]
+    for t, load in enumerate(loads):
+        load.wait()
+        for k in range(NX):
+            fs[t, k] = fv[t, :, KX * k : KX * (k + 1)]
+    own_head = wk.at[:, shard]
+    pltpu.make_async_copy(own_head, own_head, load_sems.at[0]).wait()
     pl.semaphore_wait(barrier, len(peers))
 
     odd = y - 2 * shard
@@ -514,6 +523,7 @@
     vmem = pl.BlockSpec(memory_space=pltpu.VMEM)
     smem = pl.BlockSpec(memory_space=pltpu.SMEM)
     scratch = [
+        ((2, ROWS, D), BF16),
         ((2, NX, ROWS, KX), BF16),
         ((8, ROWS, KX), BF16),
         ((CHUNKS, 2, SHARD, COLS), BF16),
@@ -566,10 +576,11 @@
             jax.ShapeDtypeStruct((2, CUT, 108), F32),
             jax.ShapeDtypeStruct((24, 128), F32),
         ),
-        in_specs=[vmem] * 8,
+        in_specs=[pl.BlockSpec(memory_space=pl.ANY)] * 4 + [vmem] * 4,
         out_specs=(vmem, vmem, vmem),
         scratch_shapes=[pltpu.VMEM(shape, dtype) for shape, dtype in scratch]
-        + [pltpu.SemaphoreType.DMA((N_GROUPS,))] * 2,
+        + [pltpu.SemaphoreType.DMA((N_GROUPS,))] * 2
+        + [pltpu.SemaphoreType.DMA((3,))],
         compiler_params=pltpu.CompilerParams(
             collective_id=0, has_side_effects=True, vmem_limit_bytes=56 * 2**20
         ),

time: 88.3 us -> 85.9 us (0.973)
  Pallas kernels: 86.2 us -> 83.8 us
    pallas_call x1, Pallas kernels: 84.2 us -> 81.7 us  [per_device(): pl.pallas_call(kernel, out_shape=(jax.ShapeDtypeStruct((2, NX, ROWS, KX),...]
where the time goes in v6:
time: 85.9 us; the launch traced here: 85.7 us
  Pallas kernels  83.8 us (98%)
  between operations  1.93 us (2%)
    pallas_call x1, Pallas kernels, per_device(): pl.pallas_call(kernel, out_shape=(jax.ShapeDtypeStruct((2, NX, ROWS, KX),...  81.7 us
    pallas_call x1, Pallas kernels, per_device(): pl.pallas_call(finish, out_shape=(jax.ShapeDtypeStruct((1,), F32), jax.Sh...  2.02 us

profile of v6, /device:TPU:1, one launch (start us, length us, event | category | flops | bytes accessed | tf_op | source)
XLA Modules:
  0.0 85.7 jit_solution(3090964991070922387)
XLA Ops:
  1.9 81.7 %shard_map.135 = (bf16[2,4,32,288]{3,2,1,0:T(8,128)(2,1)}, f32[2,48,108]{2,1,0:T(8,128)}, f32[24,128]{1,0:T(8,128)}) custom-call(bf16[32,1152]{1,0:T(8,128)(2,1)} %f_img.1, bf16[32,1152]{1,0:T(8,128)(2,1)} %f_txt.1, bf16[144,1152]{1,0:T(8,128)(2,1)} %w_img.1, bf16[144,1152]{1,0:T(8,128)(2,1)} %w_txt.1, f32[1152]{0:T(1024)} %b_img.1, f32[1152]{0:T(1024)} %b_txt.1, ...), custom_call_target="tpu_custom_call" | custom-call | tf_op jit(solution)/shard_map/pallas_call | solution.py:572
  83.7 2.0 %shard_map.136 = (f32[1]{0:T(128)}, f32[2]{0:T(128)}, bf16[32,1152]{1,0:T(8,128)(2,1)}, bf16[32,1152]{1,0:T(8,128)(2,1)}, f32[36,144]{1,0:T(8,128)}, /*index=5*/f32[36,144]{1,0:T(8,128)}, f32[2,1152]{1,0:T(2,128)}) custom-call(bf16[2,4,32,288]{3,2,1,0:T(8,128)(2,1)} %get-tuple-element.17.rf, f32[2,48,108]{2,1,0:T(8,128)} %get-tuple-element.18.ow, ...), custom_call_target="tpu_custom_call" | custom-call | tf_op jit(solution)/shard_map/pallas_call | solution.py:588

commit v7 on v6

--- a/solution.py
+++ b/solution.py
@@ -48,8 +48,9 @@
         self.y_dp = [(v - 2 * h) * 16 for v, h in zip(self.ys, self.y_mp)]
         self.z_dp = [2 * v for v in self.zs]
 
-    def at(self, dx=0, dy=0, dz=0, dc=0):
-        return (self.y_dp[dy] + self.z_dp[dz] + self.cs[dc], self.x_mp[dx] + self.y_mp[dy])
+    def at(self, dx=0, dy=0, dz=0, dc=0, core=None):
+        core = self.cs[dc] if core is None else core
+        return (self.y_dp[dy] + self.z_dp[dz] + core, self.x_mp[dx] + self.y_mp[dy])
 
     def group(self, region):
         copies = Group(self, len(self.started), region)
@@ -217,10 +218,10 @@
 def kernel(
     f_img, f_txt, w_img, w_txt, b_img, b_txt, log_scale, logit_bias,
     rf, ow, o_sums,
-    fv, fs, fk, wk, po, pk, rp0, rp, unit, inv, ia, ta, wt, wn, tg, tgx, tgs, tz_sent, tz_got,
+    fv, bv_img, bv_txt, fs, fk, wk, po, pk, rp0, rp, unit, inv, ia, ta, wt, wn, tg, tgx, tgs, tz_sent, tz_got,
     ig0, ig_x32, ig_y32, ig_top, ig_low, r_top, r_low, ig2_top, ig2_low, r2_top, r2_low,
     d16, dk, bp, bx, by, bz, bs, dfs, g32, gy, ry, gz32, gz_sent, gz_got, gz_own,
-    send_sems, recv_sems, load_sems,
+    send_sems, recv_sems, load_sems, scalars,
 ):
     link = Links(send_sems, recv_sems)
     x, y, z, c = link.x, link.y, link.z, link.c
@@ -237,6 +238,11 @@
     loads = [
         pltpu.make_async_copy(f, fv.at[t], load_sems.at[1 + t]) for t, f in enumerate((f_img, f_txt))
     ]
+    small = ((log_scale, scalars.at[0]), (logit_bias, scalars.at[1]), (b_img, bv_img), (b_txt, bv_txt))
+    small_loads = [
+        pltpu.make_async_copy(v, place, load_sems.at[3 + k]) for k, (v, place) in enumerate(small)
+    ]
+    loads += small_loads
     for load in loads:
         load.start()
 
@@ -248,12 +254,14 @@
     for p in peers:
         pl.semaphore_signal(barrier, inc=1, device_id=link.at(*p), device_id_type=MESH)
 
-    for t, load in enumerate(loads):
-        load.wait()
+    for t in range(2):
+        loads[t].wait()
         for k in range(NX):
             fs[t, k] = fv[t, :, KX * k : KX * (k + 1)]
     own_head = wk.at[:, shard]
     pltpu.make_async_copy(own_head, own_head, load_sems.at[0]).wait()
+    for load in small_loads:
+        load.wait()
     pl.semaphore_wait(barrier, len(peers))
 
     odd = y - 2 * shard
@@ -290,7 +298,7 @@
     for k in range(CHUNKS):
         wait_all(got_p[k])
         cols = slice(COLS * k, COLS * (k + 1))
-        for t, bias in enumerate((b_img, b_txt)):
+        for t, bias in enumerate((bv_img, bv_txt)):
             e = link.cs[t]
             pre = rp0[k, e] + bias[cols].reshape(1, COLS)
             for r in range(NX - 1):
@@ -313,8 +321,8 @@
     interleave(gather_z(link, ta.at[0], HALF, forward), gather_plane(link, ia))
 
     half = NZ * ROWS
-    scale = jnp.exp(log_scale[...].reshape(1, 1))
-    shift = logit_bias[...].reshape(1, 1)
+    scale = jnp.exp(jnp.full((1, 1), scalars[0, 0], F32))
+    shift = scalars[1, 0]
     images = ia[...].reshape(16 * ROWS, E)
     stats = []
     for h in range(2):
@@ -388,17 +396,10 @@
         ig2_top[i - 1] = total.astype(BF16)
         got_top2.send(ig2_top.at[i - 1], r2_top.at[i - 1], link.at(dx=i))
 
-    grad_txt = reduce_z_sum(txt_part, tz_got, got_tg)
-    got_low2.wait_recv()
-    got_top2.wait_recv()
-    halves = []
-    for rows, first_got, second_got in ((top, r_top, r2_top), (low, r_low, r2_low)):
-        total = ig0[rows, :]
-        for k in range(3):
-            total = total + first_got[k, 0].astype(F32) + second_got[k].astype(F32)
-        halves.append(total)
-    grad_img = jnp.concatenate(halves, axis=0)
-    for t, grad in enumerate((grad_img, grad_txt)):
+    got_b = link.group(bx)
+    got_d = [link.group(dk.at[h, 1:]) for h in range(2)]
+
+    def norm_backward(t, grad):
         grad = scale * grad
         delta = inv[t, :, 0:1] * (grad - unit[t] * jnp.sum(unit[t] * grad, axis=1, keepdims=True))
         for h in range(2):
@@ -408,27 +409,41 @@
         total = jnp.sum(delta, axis=0, keepdims=True)
         for k in range(9):
             bp[9 * t + k : 9 * t + k + 1, :] = total[:, 128 * k : 128 * (k + 1)]
+
+    def send_deltas(t):
+        for h in range(2):
+            for r in (2, 1, 3):
+                slot = (NX - r) * 2 + link.cs[t]
+                got_d[h].send(d16.at[h, t], dk.at[h, slot], link.at(dx=r, core=t))
+
+            @pl.when(c == t)
+            def _():
+                dk[h, 0] = d16[h, t]
+
+            @pl.when(c != t)
+            def _():
+                got_d[h].send(d16.at[h, t], dk.at[h, 1], link.at(dc=1))
+
+    norm_backward(1, reduce_z_sum(txt_part, tz_got, got_tg))
+    send_deltas(1)
+    got_low2.wait_recv()
+    got_top2.wait_recv()
+    halves = []
+    for rows, first_got, second_got in ((top, r_top, r2_top), (low, r_low, r2_low)):
+        total = ig0[rows, :]
+        for k in range(3):
+            total = total + first_got[k, 0].astype(F32) + second_got[k].astype(F32)
+        halves.append(total)
+    norm_backward(0, jnp.concatenate(halves, axis=0))
     for k in range(3):
         lanes = stats[0][k] + stats[1][k]
         bp[18 + k : 19 + k, :] = (
             lanes[:, 0:128] + lanes[:, 128:256] + lanes[:, 256:384] + lanes[:, 384:512]
         )
     bp[21:24, :] = jnp.zeros((3, 128), F32)
-
-    got_b = link.group(bx)
     for r in range(1, NX):
         got_b.send(bp, bx.at[r - 1], link.at(dx=r))
-    got_d = []
-    for h in range(2):
-        got_d.append(link.group(dk.at[h, 1:]))
-        for r in (0, 2, 1, 3):
-            for e in range(2):
-                if (r, e) == (0, 0):
-                    dk[h, 0] = d16[h, c]
-                    continue
-                got_d[h].send(
-                    d16.at[h, link.cs[e]], dk.at[h, ((NX - r) % NX) * 2 + e], link.at(dx=r, dc=e)
-                )
+    send_deltas(0)
     got_b.wait_recv()
     by[0] = bp[...] + bx[0] + bx[1] + bx[2]
     got_b = link.group(by.at[1:])
@@ -520,10 +535,13 @@
 
 
 def per_device(f_img, f_txt, w_img, w_txt, b_img, b_txt, log_scale, logit_bias):
+    hbm = pl.BlockSpec(memory_space=pl.ANY)
     vmem = pl.BlockSpec(memory_space=pltpu.VMEM)
     smem = pl.BlockSpec(memory_space=pltpu.SMEM)
     scratch = [
         ((2, ROWS, D), BF16),
+        ((E,), F32),
+        ((E,), F32),
         ((2, NX, ROWS, KX), BF16),
         ((8, ROWS, KX), BF16),
         ((CHUNKS, 2, SHARD, COLS), BF16),
@@ -576,11 +594,11 @@
             jax.ShapeDtypeStruct((2, CUT, 108), F32),
             jax.ShapeDtypeStruct((24, 128), F32),
         ),
-        in_specs=[pl.BlockSpec(memory_space=pl.ANY)] * 4 + [vmem] * 4,
+        in_specs=[hbm] * 8,
         out_specs=(vmem, vmem, vmem),
         scratch_shapes=[pltpu.VMEM(shape, dtype) for shape, dtype in scratch]
         + [pltpu.SemaphoreType.DMA((N_GROUPS,))] * 2
-        + [pltpu.SemaphoreType.DMA((3,))],
+        + [pltpu.SemaphoreType.DMA((7,)), pltpu.SMEM((2, 1), F32)],
         compiler_params=pltpu.CompilerParams(
             collective_id=0, has_side_effects=True, vmem_limit_bytes=56 * 2**20
         ),

time: 85.9 us -> 84.4 us (0.983)
  Pallas kernels: 83.8 us -> 82.3 us
    pallas_call x1, Pallas kernels: 81.7 us -> 80.3 us  [per_device(): pl.pallas_call(kernel, out_shape=(jax.ShapeDtypeStruct((2, NX, ROWS, KX),...]
where the time goes in v7:
time: 84.4 us; the launch traced here: 84.2 us
  Pallas kernels  82.3 us (98%)
  between operations  1.93 us (2%)
    pallas_call x1, Pallas kernels, per_device(): pl.pallas_call(kernel, out_shape=(jax.ShapeDtypeStruct((2, NX, ROWS, KX),...  80.3 us
    pallas_call x1, Pallas kernels, per_device(): pl.pallas_call(finish, out_shape=(jax.ShapeDtypeStruct((1,), F32), jax.Sh...  2.02 us

profile of v7, /device:TPU:1, one launch (start us, length us, event | category | flops | bytes accessed | tf_op | source)
XLA Modules:
  0.0 84.2 jit_solution(6660803611865904595)
XLA Ops:
  1.9 80.3 %shard_map.135 = (bf16[2,4,32,288]{3,2,1,0:T(8,128)(2,1)}, f32[2,48,108]{2,1,0:T(8,128)}, f32[24,128]{1,0:T(8,128)}) custom-call(bf16[32,1152]{1,0:T(8,128)(2,1)} %f_img.1, bf16[32,1152]{1,0:T(8,128)(2,1)} %f_txt.1, bf16[144,1152]{1,0:T(8,128)(2,1)} %w_img.1, bf16[144,1152]{1,0:T(8,128)(2,1)} %w_txt.1, f32[1152]{0:T(1024)} %b_img.1, f32[1152]{0:T(1024)} %b_txt.1, ...), custom_call_target="tpu_custom_call" | custom-call | tf_op jit(solution)/shard_map/pallas_call | solution.py:590
  82.2 2.0 %shard_map.136 = (f32[1]{0:T(128)}, f32[2]{0:T(128)}, bf16[32,1152]{1,0:T(8,128)(2,1)}, bf16[32,1152]{1,0:T(8,128)(2,1)}, f32[36,144]{1,0:T(8,128)}, /*index=5*/f32[36,144]{1,0:T(8,128)}, f32[2,1152]{1,0:T(2,128)}) custom-call(bf16[2,4,32,288]{3,2,1,0:T(8,128)(2,1)} %get-tuple-element.17.rf, f32[2,48,108]{2,1,0:T(8,128)} %get-tuple-element.18.ow, ...), custom_call_target="tpu_custom_call" | custom-call | tf_op jit(solution)/shard_map/pallas_call | solution.py:606

commit v8 on v7

--- a/solution.py
+++ b/solution.py
@@ -217,8 +217,8 @@
 
 def kernel(
     f_img, f_txt, w_img, w_txt, b_img, b_txt, log_scale, logit_bias,
-    rf, ow, o_sums,
-    fv, bv_img, bv_txt, fs, fk, wk, po, pk, rp0, rp, unit, inv, ia, ta, wt, wn, tg, tgx, tgs, tz_sent, tz_got,
+    o_loss, o_scale, o_fi, o_ft, o_wi, o_wt, o_bias,
+    rf, ow, fv, bv_img, bv_txt, fs, fk, wk, po, pk, rp0, rp, unit, inv, ia, ta, wt, wn, tg, tgx, tgs, tz_sent, tz_got,
     ig0, ig_x32, ig_y32, ig_top, ig_low, r_top, r_low, ig2_top, ig2_low, r2_top, r2_low,
     d16, dk, bp, bx, by, bz, bs, dfs, g32, gy, ry, gz32, gz_sent, gz_got, gz_own,
     send_sems, recv_sems, load_sems, scalars,
@@ -360,17 +360,19 @@
     top, low = pl.ds(0, HALF), pl.ds(HALF, HALF)
     texts = ta[...].reshape(16 * ROWS, E)
     got_low, got_top = link.group(r_low), link.group(r_top)
-    for i, a in enumerate((2, 1, 3, 0)):
-        grad = matmul(wt[128 * a : 128 * (a + 1), :], texts).reshape(NY, ROWS, E)
-        ig_top[:, a] = grad[:, :HALF].astype(BF16)
-        ig_low[a] = grad[:, HALF:].astype(BF16)
-        if a:
-            ig_x32[a - 1] = grad[0, :HALF]
-            got_low.send(ig_low.at[a], r_low.at[a - 1], link.at(dx=a))
-        else:
-            ig0[...] = grad[0]
-            ig_y32[...] = grad[1:, HALF:]
-        if i == 0:
+    for pair in ((1, 2), (3, 0)):
+        w_rows = [wt[NY * ROWS * a : NY * ROWS * (a + 1), :] for a in pair]
+        grads = matmul(jnp.concatenate(w_rows, axis=0), texts).reshape(2, NY, ROWS, E)
+        for a, grad in zip(pair, (grads[0], grads[1])):
+            ig_top[:, a] = grad[:, :HALF].astype(BF16)
+            ig_low[a] = grad[:, HALF:].astype(BF16)
+            if a:
+                ig_x32[a - 1] = grad[0, :HALF]
+                got_low.send(ig_low.at[a], r_low.at[a - 1], link.at(dx=a))
+            else:
+                ig0[...] = grad[0]
+                ig_y32[...] = grad[1:, HALF:]
+        if 0 not in pair:
             tg[...] = matmul(wn[...], images).reshape(NZ, ROWS, E)
             got_x[0].wait_recv()
             first = reduce_z_start(link, txt_part, tz_sent, tz_got, HALF)
@@ -465,6 +467,13 @@
         got_y.append(link.group(ry.at[h]))
         for j in (2, 1, 3):
             got_y[h].send(gy.at[h, link.ys[j]], ry.at[h, j - 1], link.at(dy=j))
+        if h == 0:
+            got_b.wait_recv()
+            bz[0] = by[0] + by[1] + by[2] + by[3]
+            sums = gather_z(link, bz, None, lambda k: None)
+            next(sums)
+    next(sums)
+    next(sums)
 
     deltas = jnp.concatenate([d[:, QUARTER * q : QUARTER * (q + 1)] for q in range(2) for d in deltas], axis=1)
     grad_f = 0.0
@@ -479,14 +488,6 @@
                 continue
             got_df.send(dfs.at[r * 2 + e], rf.at[e, x], link.at(dx=r, dc=e))
 
-    got_b.wait_recv()
-    bz[0] = by[0] + by[1] + by[2] + by[3]
-    interleave(gather_z(link, bz, None, lambda k: None))
-    bias_sum = bz[0]
-    for k in range(1, NZ):
-        bias_sum = bias_sum + bz[k]
-    bs[0] = bias_sum
-    got_b = link.send(bs.at[0], bs.at[1], link.at(dc=1))
 
     for h in range(2):
         got_y[h].wait_recv()
@@ -498,40 +499,56 @@
                 col = 72 * k + 36 * e
                 block = [total[:, QUARTER * i + col : QUARTER * i + col + 36] for i in range(3)]
                 gz32[NZ // 2 * h + k, e] = jnp.concatenate(block, axis=1)
+        if h == 0:
+            interleave(sums)
+            bias_sum = bz[0]
+            for k in range(1, NZ):
+                bias_sum = bias_sum + bz[k]
+            bs[0] = bias_sum
+            got_b = link.send(bs.at[0], bs.at[1], link.at(dc=1))
 
     def head_part(k):
         return gz32[link.zs[k]]
 
     first = reduce_z_start(link, head_part, gz_sent, gz_got, 1)
     got_own = link.send(gz32.at[z, link.cs[1]], gz_own, link.at(dc=1))
+    got_df.wait_recv()
+    for t, out in enumerate((o_fi, o_ft)):
+        for k in range(NX):
+            out[:, KX * k : KX * (k + 1)] = rf[link.cs[t], k]
     last = reduce_z_finish(link, head_part, gz_sent, gz_got, 1, first, over_cores=True)
+    got_b.wait_recv()
+    sums = bs[0] + bs[1]
+    for t in range(2):
+        for k in range(9):
+            o_bias[t : t + 1, 128 * k : 128 * (k + 1)] = sums[9 * t + k : 9 * t + k + 1, :]
+    o_loss[0] = jnp.sum(sums[18:19, :]) * (1.0 / 8192.0)
+    o_scale[0] = jnp.sum(sums[19:20, :])
+    o_scale[1] = jnp.sum(sums[20:21, :])
     got_own.wait_recv()
     wait_all(last)
     for e, total in enumerate((gz32[z, c], gz_own[...])):
         for i in range(4):
             total = total + gz_got[3 + i, e].astype(F32)
         ow[e] = total
-    got_b.wait_recv()
-    o_sums[...] = bs[0] + bs[1]
-    got_df.wait_recv()
+    for t, out in enumerate((o_wi, o_wt)):
+        block = ow[link.cs[t]]
+        for k in range(3):
+            out[:, CUT * k : CUT * (k + 1)] = block[:, 36 * k : 36 * (k + 1)].T
 
     for copy in link.started:
         copy.wait_send()
 
 
-def finish(rf, ow, sums, o_loss, o_scale, o_fi, o_ft, o_wi, o_wt, o_bias):
-    c = lax.axis_index("dp") % 2
-    for t, (out_f, out_w) in enumerate(((o_fi, o_wi), (o_ft, o_wt))):
-        e = jnp.where(c == t, 0, 1)
-        for k in range(NX):
-            out_f[:, KX * k : KX * (k + 1)] = rf[e, k]
-        for k in range(3):
-            out_w[:, CUT * k : CUT * (k + 1)] = ow[e][:, 36 * k : 36 * (k + 1)].T
-        for k in range(9):
-            o_bias[t : t + 1, 128 * k : 128 * (k + 1)] = sums[9 * t + k : 9 * t + k + 1, :]
-    o_loss[0] = jnp.sum(sums[18:19, :]) * (1.0 / 8192.0)
-    o_scale[0] = jnp.sum(sums[19:20, :])
-    o_scale[1] = jnp.sum(sums[20:21, :])
+def finish(*refs):
+    parts, outs, sems = refs[:7], refs[7:14], refs[14]
+    copies = [
+        pltpu.make_async_copy(part, out, sems.at[k]) for k, (part, out) in enumerate(zip(parts, outs))
+    ]
+    for copy in copies:
+        copy.start()
+    for copy in copies:
+        copy.wait()
 
 
 def per_device(f_img, f_txt, w_img, w_txt, b_img, b_txt, log_scale, logit_bias):
@@ -539,6 +556,8 @@
     vmem = pl.BlockSpec(memory_space=pltpu.VMEM)
     smem = pl.BlockSpec(memory_space=pltpu.SMEM)
     scratch = [
+        ((2, NX, ROWS, KX), BF16),
+        ((2, CUT, 108), F32),
         ((2, ROWS, D), BF16),
         ((E,), F32),
         ((E,), F32),
@@ -587,15 +606,20 @@
         ((7, 2, CUT, 108), BF16),
         ((CUT, 108), F32),
     ]
+    shapes = (
+        jax.ShapeDtypeStruct((1,), F32),
+        jax.ShapeDtypeStruct((2,), F32),
+        jax.ShapeDtypeStruct((ROWS, D), BF16),
+        jax.ShapeDtypeStruct((ROWS, D), BF16),
+        jax.ShapeDtypeStruct((36, SHARD), F32),
+        jax.ShapeDtypeStruct((36, SHARD), F32),
+        jax.ShapeDtypeStruct((2, E), F32),
+    )
     parts = pl.pallas_call(
         kernel,
-        out_shape=(
-            jax.ShapeDtypeStruct((2, NX, ROWS, KX), BF16),
-            jax.ShapeDtypeStruct((2, CUT, 108), F32),
-            jax.ShapeDtypeStruct((24, 128), F32),
-        ),
+        out_shape=shapes,
         in_specs=[hbm] * 8,
-        out_specs=(vmem, vmem, vmem),
+        out_specs=(smem, smem, vmem, vmem, vmem, vmem, vmem),
         scratch_shapes=[pltpu.VMEM(shape, dtype) for shape, dtype in scratch]
         + [pltpu.SemaphoreType.DMA((N_GROUPS,))] * 2
         + [pltpu.SemaphoreType.DMA((7,)), pltpu.SMEM((2, 1), F32)],
@@ -605,17 +629,10 @@
     )(f_img, f_txt, w_img, w_txt, b_img, b_txt, log_scale, logit_bias)
     loss, scale, fi, ft, wi, wt, bias = pl.pallas_call(
         finish,
-        out_shape=(
-            jax.ShapeDtypeStruct((1,), F32),
-            jax.ShapeDtypeStruct((2,), F32),
-            jax.ShapeDtypeStruct((ROWS, D), BF16),
-            jax.ShapeDtypeStruct((ROWS, D), BF16),
-            jax.ShapeDtypeStruct((36, SHARD), F32),
-            jax.ShapeDtypeStruct((36, SHARD), F32),
-            jax.ShapeDtypeStruct((2, E), F32),
-        ),
-        in_specs=[vmem] * 3,
-        out_specs=(smem, smem, vmem, vmem, vmem, vmem, vmem),
+        out_shape=shapes,
+        in_specs=[hbm] * 7,
+        out_specs=(hbm,) * 7,
+        scratch_shapes=[pltpu.SemaphoreType.DMA((7,))],
     )(*parts)
     return loss, scale, fi, ft, wi.T, wt.T, bias
 

time: 84.4 us -> 91.6 us (1.085)
  Pallas kernels: 82.3 us -> 89.5 us
    pallas_call x2, Pallas kernels: 82.3 us -> 89.5 us  [the longest x1 80.4 us: per_device(): pl.pallas_call(kernel, out_shape=shapes, in_specs=[hbm] * 8, out_specs=(s...]
where the time goes in v8:
time: 91.6 us; the launch traced here: 91.4 us
  Pallas kernels  89.5 us (98%)
  between operations  1.93 us (2%)
    pallas_call x1, Pallas kernels, per_device(): pl.pallas_call(kernel, out_shape=shapes, in_specs=[hbm] * 8, out_specs=(s...  80.4 us
    pallas_call x1, Pallas kernels, per_device(): pl.pallas_call(finish, out_shape=shapes, in_specs=[hbm] * 7, out_specs=(h...  9.09 us

profile of v8, /device:TPU:1, one launch (start us, length us, event | category | flops | bytes accessed | tf_op | source)
XLA Modules:
  0.0 91.4 jit_solution(10421873382319024990)
XLA Ops:
  1.9 80.4 %shard_map.135 = (f32[1]{0:T(128)}, f32[2]{0:T(128)}, bf16[32,1152]{1,0:T(8,128)(2,1)}, bf16[32,1152]{1,0:T(8,128)(2,1)}, f32[36,144]{1,0:T(8,128)}, /*index=5*/f32[36,144]{1,0:T(8,128)}, f32[2,1152]{1,0:T(2,128)}) custom-call(bf16[32,1152]{1,0:T(8,128)(2,1)} %f_img.1, bf16[32,1152]{1,0:T(8,128)(2,1)} %f_txt.1, bf16[144,1152]{1,0:T(8,128)(2,1)} %w_img.1, ...), custom_call_target="tpu_custom_call" | custom-call | tf_op jit(solution)/shard_map/pallas_call | solution.py:618
  82.3 9.1 %shard_map.136 = (f32[1]{0:T(128)}, f32[2]{0:T(128)}, bf16[32,1152]{1,0:T(8,128)(2,1)}, bf16[32,1152]{1,0:T(8,128)(2,1)}, f32[36,144]{1,0:T(8,128)}, /*index=5*/f32[36,144]{1,0:T(8,128)}, f32[2,1152]{1,0:T(2,128)}) custom-call(f32[1]{0:T(128)} %get-tuple-element.21.refs_0_, f32[2]{0:T(128)} %get-tuple-element.22.refs_1_, ...), custom_call_target="tpu_custom_call" | custom-call | tf_op jit(solution)/shard_map/pallas_call | solution.py:630

commit v9 on v7

--- a/solution.py
+++ b/solution.py
@@ -348,29 +348,31 @@
         wt[:, half * h : half * (h + 1)] = weights.T
         if h == 0:
             wn[...] = weights
-    tgx[...] = matmul(weights, images).reshape(NZ, ROWS, E)
+    tgx[...] = matmul(weights, images).astype(BF16).reshape(NZ, ROWS, E)
     got_x = [
         link.send(tgx.at[k], tgs.at[k], link.at(dc=1))
         for k in (pl.ds(3, 3), pl.ds(0, 3), pl.ds(6, 2))
     ]
 
     def txt_part(k):
-        return tg[k] + tgs[k]
+        return tg[k] + tgs[k].astype(F32)
 
     top, low = pl.ds(0, HALF), pl.ds(HALF, HALF)
     texts = ta[...].reshape(16 * ROWS, E)
     got_low, got_top = link.group(r_low), link.group(r_top)
-    for i, a in enumerate((2, 1, 3, 0)):
-        grad = matmul(wt[128 * a : 128 * (a + 1), :], texts).reshape(NY, ROWS, E)
-        ig_top[:, a] = grad[:, :HALF].astype(BF16)
-        ig_low[a] = grad[:, HALF:].astype(BF16)
-        if a:
-            ig_x32[a - 1] = grad[0, :HALF]
-            got_low.send(ig_low.at[a], r_low.at[a - 1], link.at(dx=a))
-        else:
-            ig0[...] = grad[0]
-            ig_y32[...] = grad[1:, HALF:]
-        if i == 0:
+    for pair in ((1, 2), (3, 0)):
+        w_rows = [wt[NY * ROWS * a : NY * ROWS * (a + 1), :] for a in pair]
+        grads = matmul(jnp.concatenate(w_rows, axis=0), texts).reshape(2, NY, ROWS, E)
+        for a, grad in zip(pair, (grads[0], grads[1])):
+            ig_top[:, a] = grad[:, :HALF].astype(BF16)
+            ig_low[a] = grad[:, HALF:].astype(BF16)
+            if a:
+                ig_x32[a - 1] = grad[0, :HALF]
+                got_low.send(ig_low.at[a], r_low.at[a - 1], link.at(dx=a))
+            else:
+                ig0[...] = grad[0]
+                ig_y32[...] = grad[1:, HALF:]
+        if 0 not in pair:
             tg[...] = matmul(wn[...], images).reshape(NZ, ROWS, E)
             got_x[0].wait_recv()
             first = reduce_z_start(link, txt_part, tz_sent, tz_got, HALF)
@@ -465,6 +467,13 @@
         got_y.append(link.group(ry.at[h]))
         for j in (2, 1, 3):
             got_y[h].send(gy.at[h, link.ys[j]], ry.at[h, j - 1], link.at(dy=j))
+        if h == 0:
+            got_b.wait_recv()
+            bz[0] = by[0] + by[1] + by[2] + by[3]
+            sums = gather_z(link, bz, None, lambda k: None)
+            next(sums)
+    next(sums)
+    next(sums)
 
     deltas = jnp.concatenate([d[:, QUARTER * q : QUARTER * (q + 1)] for q in range(2) for d in deltas], axis=1)
     grad_f = 0.0
@@ -479,14 +488,6 @@
                 continue
             got_df.send(dfs.at[r * 2 + e], rf.at[e, x], link.at(dx=r, dc=e))
 
-    got_b.wait_recv()
-    bz[0] = by[0] + by[1] + by[2] + by[3]
-    interleave(gather_z(link, bz, None, lambda k: None))
-    bias_sum = bz[0]
-    for k in range(1, NZ):
-        bias_sum = bias_sum + bz[k]
-    bs[0] = bias_sum
-    got_b = link.send(bs.at[0], bs.at[1], link.at(dc=1))
 
     for h in range(2):
         got_y[h].wait_recv()
@@ -498,6 +499,13 @@
                 col = 72 * k + 36 * e
                 block = [total[:, QUARTER * i + col : QUARTER * i + col + 36] for i in range(3)]
                 gz32[NZ // 2 * h + k, e] = jnp.concatenate(block, axis=1)
+        if h == 0:
+            interleave(sums)
+            bias_sum = bz[0]
+            for k in range(1, NZ):
+                bias_sum = bias_sum + bz[k]
+            bs[0] = bias_sum
+            got_b = link.send(bs.at[0], bs.at[1], link.at(dc=1))
 
     def head_part(k):
         return gz32[link.zs[k]]
@@ -556,8 +564,8 @@
         ((512, 512), BF16),
         ((256, 512), BF16),
         ((NZ, ROWS, E), F32),
-        ((NZ, ROWS, E), F32),
-        ((NZ, ROWS, E), F32),
+        ((NZ, ROWS, E), BF16),
+        ((NZ, ROWS, E), BF16),
         ((7, ROWS, E), BF16),
         ((7, ROWS, E), BF16),
         ((ROWS, E), F32),

time: 84.4 us -> 83.7 us (level)
  no operation moved by 1% of the time
where the time goes in v9:
time: 83.7 us; the launch traced here: 83.5 us
  Pallas kernels  81.6 us (97%)
  between operations  1.93 us (2%)
    pallas_call x1, Pallas kernels, per_device(): pl.pallas_call(kernel, out_shape=(jax.ShapeDtypeStruct((2, NX, ROWS, KX),...  79.6 us
    pallas_call x1, Pallas kernels, per_device(): pl.pallas_call(finish, out_shape=(jax.ShapeDtypeStruct((1,), F32), jax.Sh...  2.02 us

profile of v9, /device:TPU:1, one launch (start us, length us, event | category | flops | bytes accessed | tf_op | source)
XLA Modules:
  0.0 83.5 jit_solution(14632172294583219814)
XLA Ops:
  1.9 79.6 %shard_map.135 = (bf16[2,4,32,288]{3,2,1,0:T(8,128)(2,1)}, f32[2,48,108]{2,1,0:T(8,128)}, f32[24,128]{1,0:T(8,128)}) custom-call(bf16[32,1152]{1,0:T(8,128)(2,1)} %f_img.1, bf16[32,1152]{1,0:T(8,128)(2,1)} %f_txt.1, bf16[144,1152]{1,0:T(8,128)(2,1)} %w_img.1, bf16[144,1152]{1,0:T(8,128)(2,1)} %w_txt.1, f32[1152]{0:T(1024)} %b_img.1, f32[1152]{0:T(1024)} %b_txt.1, ...), custom_call_target="tpu_custom_call" | custom-call | tf_op jit(solution)/shard_map/pallas_call | solution.py:598
  81.5 2.0 %shard_map.136 = (f32[1]{0:T(128)}, f32[2]{0:T(128)}, bf16[32,1152]{1,0:T(8,128)(2,1)}, bf16[32,1152]{1,0:T(8,128)(2,1)}, f32[36,144]{1,0:T(8,128)}, /*index=5*/f32[36,144]{1,0:T(8,128)}, f32[2,1152]{1,0:T(2,128)}) custom-call(bf16[2,4,32,288]{3,2,1,0:T(8,128)(2,1)} %get-tuple-element.17.rf, f32[2,48,108]{2,1,0:T(8,128)} %get-tuple-element.18.ow, ...), custom_call_target="tpu_custom_call" | custom-call | tf_op jit(solution)/shard_map/pallas_call | solution.py:614
